TPU v7x, 256 devices: a whole 4x4x8 slice. The times are simulated.
256 devices in a mesh: items: 16 (over z_hi, x), events: 16 (over y, z_lo, core).
Axes of the slice: x: 4, y: 4, z: 8 (z_hi: 4, z_lo: 2; z = z_hi * 2 + z_lo), core: 2. Of those that a mesh axis runs over, the one named last changes fastest.
Arguments:
- history: bfloat16 [16, 2048, 1024], P('items', 'events'), may hold values from -6 to 6
- actions: int32 [16, 2048], P('items', 'events'), may hold values from 0 to 15
- action_table: bfloat16 [16, 1024], replicated, may hold values from -3 to 3
- lengths: int32 [16], P('items'), may hold values from 512 to 2048, as said below
- input_gain: float32 [1024], replicated, may hold values from 0.25 to 1.75
- input_weight: bfloat16 [1024, 4096], replicated, may hold values from -0.1875 to 0.1875
- output_gain: float32 [1024], replicated, may hold values from 0.25 to 1.75
- output_weight: bfloat16 [1024, 1024], replicated, may hold values from -0.1875 to 0.1875
- item_codes: int32 [32768, 256], P(('items', 'events')), may hold values from 0 to 65535
- item_scale: float32 [32768, 8], P(('items', 'events')), may hold values from 0.006 to 0.06
- gate_first: bfloat16 [64, 128], replicated, may hold values from -0.75 to 0.75
- gate_second: bfloat16 [128, 64], replicated, may hold values from -0.5 to 0.5
- teacher: float32 [16, 32768], P(None, ('items', 'events')), may hold values from -12 to 12
Outputs:
- layer_out: bfloat16 [16, 2048, 1024], P('items', 'events')
- scores: float32 [16, 32768], P(None, ('items', 'events'))
- dvalues: float32 [16, 2048, 1024], P('items', 'events')
Inputs may be any that keep to these rules, and one draw needn't show every extreme that they name: `lengths`: each user's real events; later positions are padding. `item_codes`: each word holds four codes of 0 to 15, code n of word w being floor(word / 16^n) mod 16, for feature 4 w + n.
All inputs are finite; a program needn't handle non-finite values.
Results may differ from a plain program's by a relative error of at most 0.011.
Values may be sent and summed in bfloat16 or wider, within the bound.
A program may use at most 128 MiB of HBM per device.

v0:
```python
import jax
import jax.numpy as jnp
from jax import lax
from jax.sharding import PartitionSpec as P

HEADS = 8
COMPS = 8
ITEM_COMPS = 8
LENGTH = 2048


epsilon = 1e-05
highest = lax.Precision.HIGHEST


def sigmoid_linear(value_in):
    return value_in * jax.nn.sigmoid(value_in)


def sigmoid_linear_slope(value_in):
    sigmoid_v = jax.nn.sigmoid(value_in)
    return sigmoid_v * (1.0 + value_in * (1.0 - sigmoid_v))


def layer_norm(value_in, gain):
    center = value_in - jnp.mean(value_in, axis=-1, keepdims=True)
    spread = lax.rsqrt(jnp.mean(center * center, axis=-1, keepdims=True) + epsilon)
    return center * spread * gain


def dequantize(codes, scales):
    repeated = jnp.repeat(codes, 4, axis=1)
    column = jnp.arange(repeated.shape[1], dtype=jnp.int32)
    powers = (16 ** (column % 4)).astype(jnp.int32)
    nibble = repeated // powers[None, :] % 16
    comp_scale = jnp.repeat(scales, repeated.shape[1] // scales.shape[1], axis=1)
    return ((nibble.astype(jnp.float32) - 7.5) * comp_scale).astype(jnp.bfloat16)


def score_items(user_emb, item_vec, targets, gate_first, gate_second):
    user_count, width = user_emb.shape
    item_count = item_vec.shape[0]
    comp_size = width // COMPS
    user_parts = user_emb.reshape(user_count, COMPS, comp_size)
    item_parts = item_vec.reshape(item_count, ITEM_COMPS, comp_size)
    logits = jnp.einsum("bad,tcd->btac", user_parts, item_parts, preferred_element_type=jnp.float32)
    logits = logits.reshape(user_count, item_count, COMPS * ITEM_COMPS)
    first_w = gate_first.astype(jnp.float32)
    second_w = gate_second.astype(jnp.float32)
    gate_pre = jnp.einsum("btp,pk->btk", logits, first_w, precision=highest)
    gate_hidden = sigmoid_linear(gate_pre)
    gates = jax.nn.sigmoid(jnp.einsum("btk,kp->btp", gate_hidden, second_w, precision=highest))
    scores = jnp.sum(gates * logits, axis=-1)
    residual = scores - targets
    slope = gates * (1.0 - gates) * logits
    back_hidden = jnp.einsum(
        "btp,kp->btk", slope, second_w, precision=highest
    ) * sigmoid_linear_slope(gate_pre)
    dlogits = residual[:, :, None] * (
        gates + jnp.einsum("btk,pk->btp", back_hidden, first_w, precision=highest)
    )
    dembed = jnp.einsum(
        "btac,tcd->bad",
        dlogits.reshape(user_count, item_count, COMPS, ITEM_COMPS),
        item_parts.astype(jnp.float32),
        precision=highest,
    )
    return (scores, dembed.reshape(user_count, width))


def attend(key_block, value_block, query_heads, positions, lengths):
    users_here, block_len, width = key_block.shape
    head_count = query_heads.shape[2]
    head_size = width // head_count
    key_heads = key_block.reshape(users_here, block_len, head_count, head_size)
    value_heads = value_block.reshape(users_here, block_len, head_count, head_size)
    raw_scores = jnp.einsum(
        "uihd,ujhd->uhij", query_heads, key_heads, preferred_element_type=jnp.float32
    ) * head_size ** (-0.5)
    key_pos = jnp.arange(block_len, dtype=jnp.int32)
    allowed = (key_pos[None, None, :] <= positions[None, :, None]) & (
        key_pos[None, None, :] < lengths[:, None, None]
    )
    weights = jnp.where(allowed[:, None, :, :], sigmoid_linear(raw_scores) / LENGTH, 0.0).astype(
        jnp.bfloat16
    )
    return jnp.einsum("uhij,ujhd->uihd", weights, value_heads, preferred_element_type=jnp.float32)


def local(
    history,
    actions,
    action_table,
    lengths,
    input_gain,
    input_weight,
    output_gain,
    output_weight,
    item_codes,
    item_scale,
    gate_first,
    gate_second,
    teacher,
):
    users, rows, width = history.shape
    head_count = HEADS
    head_size = width // head_count
    first_row = lax.axis_index("events") * rows
    positions = first_row + jnp.arange(rows, dtype=jnp.int32)
    onehot = (
        actions[:, :, None] == jnp.arange(action_table.shape[0], dtype=jnp.int32)[None, None, :]
    ).astype(jnp.bfloat16)
    summed = history.astype(jnp.float32) + jnp.einsum(
        "usa,ad->usd", onehot, action_table, preferred_element_type=jnp.float32
    )
    normed = layer_norm(summed, input_gain).astype(jnp.bfloat16)
    projection = jnp.dot(
        normed.reshape(users * rows, width), input_weight, preferred_element_type=jnp.float32
    )
    projection = projection.reshape(users, rows, 4 * width)
    gate_u = sigmoid_linear(projection[:, :, :width])
    queries = sigmoid_linear(projection[:, :, width : 2 * width]).astype(jnp.bfloat16)
    keys = sigmoid_linear(projection[:, :, 2 * width : 3 * width]).astype(jnp.bfloat16)
    query_heads = queries.reshape(users, rows, head_count, head_size)
    pair_weight = input_weight[:, 2 * width :]
    block = lax.all_gather(normed, "events", axis=1, tiled=True)
    block_len = block.shape[1]
    pair = jnp.dot(
        block.reshape(users * block_len, width), pair_weight, preferred_element_type=jnp.float32
    )
    key_block = (
        sigmoid_linear(pair[:, :width]).astype(jnp.bfloat16).reshape(users, block_len, width)
    )
    value_block = (
        sigmoid_linear(pair[:, width:]).astype(jnp.bfloat16).reshape(users, block_len, width)
    )
    mixed = attend(key_block, value_block, query_heads, positions, lengths)
    mixed = mixed.reshape(users, rows, width)
    gated = (layer_norm(mixed, output_gain) * gate_u).astype(jnp.bfloat16)
    layer_out = summed + jnp.dot(
        gated.reshape(users * rows, width), output_weight, preferred_element_type=jnp.float32
    ).reshape(users, rows, width)
    layer_out = layer_out.astype(jnp.bfloat16)
    pick_mask = (positions[None, :] == (lengths - 1)[:, None]).astype(jnp.float32)[:, :, None]

    def at_last(field):
        return jnp.sum(pick_mask * field.astype(jnp.float32), axis=1)

    user_row, query_row, mixed_row, gate_row = lax.psum(
        (at_last(layer_out), at_last(queries), at_last(mixed), at_last(gate_u)), "events"
    )
    everyone = lax.all_gather(user_row.astype(jnp.bfloat16), "items", axis=0, tiled=True)
    item_vec = dequantize(item_codes, item_scale)
    scores, dembed_local = score_items(everyone, item_vec, teacher, gate_first, gate_second)
    grad_total = lax.psum(dembed_local, ("items", "events"))
    grad_rows = lax.dynamic_slice_in_dim(grad_total, lax.axis_index("items") * users, users, 0)
    dgated = lax.dot_general(
        grad_rows.astype(jnp.bfloat16),
        output_weight,
        (((1,), (1,)), ((), ())),
        preferred_element_type=jnp.float32,
    )
    center = mixed_row - jnp.mean(mixed_row, axis=-1, keepdims=True)
    spread = lax.rsqrt(jnp.mean(center * center, axis=-1, keepdims=True) + epsilon)
    normal = center * spread
    slope_in = dgated * gate_row * output_gain
    dmixed = (
        slope_in
        - jnp.mean(slope_in, axis=-1, keepdims=True)
        - normal * jnp.mean(slope_in * normal, axis=-1, keepdims=True)
    ) * spread
    last_query = query_row.astype(jnp.bfloat16).reshape(users, head_count, head_size)
    key_heads = keys.reshape(users, rows, head_count, head_size)
    last_scores = jnp.einsum(
        "uhd,ujhd->uhj", last_query, key_heads, preferred_element_type=jnp.float32
    ) * head_size ** (-0.5)
    keep_mask = positions[None, :] < lengths[:, None]
    last_weights = jnp.where(
        keep_mask[:, None, :], sigmoid_linear(last_scores) / LENGTH, 0.0
    ).astype(jnp.bfloat16)
    weight_cols = jnp.swapaxes(last_weights.astype(jnp.float32), 1, 2)
    dvalues = weight_cols[:, :, :, None] * dmixed.reshape(users, 1, head_count, head_size)
    return (layer_out, scores, dvalues.reshape(users, rows, width))


def solution(mesh):
    in_specs = (
        P("items", "events", None),
        P("items", "events"),
        P(),
        P("items"),
        P(),
        P(),
        P(),
        P(),
        P(("items", "events"), None),
        P(("items", "events"), None),
        P(),
        P(),
        P(None, ("items", "events")),
    )
    out_specs = (
        P("items", "events", None),
        P(None, ("items", "events")),
        P("items", "events", None),
    )
    return jax.shard_map(local, mesh=mesh, in_specs=in_specs, out_specs=out_specs, check_vma=False)
```

profile of v0, /device:TPU:1, one launch (start us, length us, event | category | flops | bytes accessed | tf_op | source)
XLA Modules:
  0.0 278.5 jit_solution(12445410933827949290)
XLA Ops:
  7.2 1.5 fusion.98
  8.9 1.5 multiply_convert_fusion.5
  10.5 1.0 copy.45
  11.5 0.9 sign.25
  13.1 4.7 %convolution_bitcast_fusion = f32[1,128,4096]{2,1,0:T(8,128)S(1)} fusion(bf16[1024,4096]{1,0:T(8,128)(2,1)} %param.18, bf16[1,128,1024]{2,1,0:T(8,128)(2,1)} %multiply_convert_fusion.5), kind=kOutput, calls=%fused_computation.3 | convolution fusion | flops 1073741824 | bytes 10747904 | tf_op jit(solution)/shard_map/dot_general | solution.py:117
  17.8 1.4 copy-done.1
  21.3 6.5 %fusion.42 = bf16[128,8,128,1]{0,2,1,3:T(8,128)(2,1)} fusion(f32[128,8]{0,1:T(8,128)S(1)} %copy-done.5, s32[8,128]{1,0:T(8,128)S(1)} %get-tuple-element.27, s32[8,128]{1,0:T(8,128)S(1)} %get-tuple-element.28, s32[128,8,128]{0,2,1:T(8,128)S(1)} %bitcast.199), kind=kLoop, calls=%fused_computation.80 | loop fusion | flops 3014656 | bytes 798720 | tf_op jit(solution)/shard_map/convert_element_type | solution.py:37
  27.8 12.0 %fusion.19 = bf16[128,256,4]{0,2,1:T(4,128)(2,1)} fusion(f32[128,256]{0,1:T(8,128)S(1)} %bitcast.203, s32[256,4]{1,0:T(8,128)S(1)} %get-tuple-element.14, s32[128,256]{0,1:T(8,128)S(1)} %copy.45, s32[256,4]{1,0:T(8,128)S(1)} %get-tuple-element.13, s32[128,256]{0,1:T(8,128)S(1)} %copy.44), kind=kLoop, calls=%fused_computation.44 | loop fusion | flops 2883584 | bytes 663552 | tf_op jit(solution)/shard_map/convert_element_type | solution.py:37
  39.8 0.9 fusion.14
  40.7 14.1 %all-gather.3.cloned.1.call-done = bf16[1,2048,1024]{2,1,0:T(8,128)(2,1)} async-done(((bf16[1,128,1024]{2,1,0:T(8,128)(2,1)}), bf16[1,2048,1024]{2,1,0:T(8,128)(2,1)}) %all-gather.3.cloned.1.call-update) | async-done | bytes 4194320 | tf_op jit(solution)/shard_map/all_gather | solution.py:126
  54.8 12.6 %fusion = f32[2048,2048]{0,1:T(8,128)S(1)} fusion(bf16[1,2048,1024]{2,1,0:T(8,128)(2,1)} %all-gather.3.cloned.1.call-done, bf16[1024,4096]{1,0:T(8,128)(2,1)} %param.18), kind=kOutput, calls=%fused_computation.4 | convolution fusion | flops 8589934592 | bytes 25165824 | tf_op jit(solution)/shard_map/dot_general | solution.py:128
  67.5 6.8 %multiply_convert_fusion = (bf16[2048,1024]{0,1:T(8,128)(2,1)}, bf16[2048,1024]{0,1:T(8,128)(2,1)}) fusion(f32[2048,2048]{0,1:T(8,128)S(1)} %fusion), kind=kLoop, calls=%fused_computation.1 | loop fusion | flops 20971520 | bytes 25165824 | tf_op jit(solution)/shard_map/convert_element_type | solution.py:132
  74.3 7.6 %fusion.99 = (f32[128]{0:T(128)S(1)}, f32[8,128,128]{2,1,0:T(8,128)S(1)}) fusion(bf16[2048,8,128]{0,2,1:T(8,128)(2,1)} %bitcast.198, bf16[2048,8,128]{0,2,1:T(8,128)(2,1)} %bitcast.197, pred[128,2048]{1,0:T(8,128)(4,1)} %fusion.14, bf16[128,8,128]{2,1,0:T(8,128)(2,1)} %bitcast.204), kind=kOutput, calls=%fused_computation.174 | convolution fusion | flops 1090649984 | bytes 9437696 | tf_op jit(solution)/shard_map/uhij,ujhd->uihd/dot_general | solution.py:87
  82.0 1.0 copy.61
  83.2 1.8 fusion.11
  85.0 2.1 multiply_reduce_fusion.1
  87.1 51.4 %all-reduce = (bf16[1,1024]{1,0:T(2,128)(2,1)S(1)}, bf16[1,1024]{1,0:T(2,128)(2,1)S(1)}, f32[1,1024]{1,0:T(1,128)S(1)}, f32[1,1024]{1,0:T(1,128)S(1)}) all-reduce(f32[1,1024]{1,0:T(1,128)S(1)} %bitcast.211, f32[1,1024]{1,0:T(1,128)S(1)} %bitcast.209, f32[1,1024]{1,0:T(1,128)S(1)} %bitcast.210, ...), channel_id=1, replica_groups=mesh['items'=16,'events'=16] {'events'}, use_global_device_ids=true, to_apply=%region_5.6 | all-reduce | flops 4096 | bytes 28672 | tf_op jit(solution)/shard_map/psum | solution.py:149
  138.5 37.2 %all-gather = bf16[16,1,1024]{2,1,0:T(2,128)(2,1)S(1)} all-gather(bf16[1,1,1024]{2,1,0:T(2,128)(2,1)S(1)} %bitcast.213), channel_id=1, replica_groups=mesh['items'=16,'events'=16] {'items'}, dimensions={0}, use_global_device_ids=true | all-gather | bytes 34816 | tf_op jit(solution)/shard_map/all_gather | solution.py:152
  179.2 1.2 convolution_bitcast_fusion.2
  180.4 1.1 fusion.30
  181.5 1.9 fusion.32
  183.4 1.2 convolution_multiply_fusion
  185.9 82.3 %psum.37 = bf16[16,1024]{1,0:T(8,128)(2,1)S(1)} all-reduce(f32[16,1024]{1,0:T(8,128)S(1)} %bitcast.205), channel_id=1, replica_groups=mesh['items'=16,'events'=16] {'items','events'}, use_global_device_ids=true, to_apply=%region_9.10 | all-reduce | flops 16384 | bytes 98304 | tf_op jit(solution)/shard_map/psum | solution.py:155
  268.1 1.3 fusion.95
  (58 shorter events, 6.6 us)
Async XLA Ops:
  7.2 76.0 %copy-start = (bf16[1024,1024]{1,0:T(8,128)(2,1)S(1)}, bf16[1024,1024]{1,0:T(8,128)(2,1)}, u32[]{:S(2)}) copy-start(bf16[1024,1024]{1,0:T(8,128)(2,1)} %param.20) | copy-start | bytes 6291460
  7.2 47.7 %all-gather.3.cloned.1.call-start = ((), (), s32[]{:S(2)}) async-start(), calls=%async_computation | async-start | bytes 4456448 | tf_op jit(solution)/shard_map/all_gather | solution.py:126
  13.1 8.2 %copy-start.5 = (f32[128,8]{0,1:T(8,128)S(1)}, f32[128,8]{0,1:T(8,128)}, u32[]{:S(2)}) copy-start(f32[128,8]{0,1:T(8,128)} %param.22) | copy-start | bytes 12292
  17.8 1.4 copy-start.1
  74.3 8.8 %copy-start.8 = (f32[1024]{0:T(1024)S(1)}, f32[1024]{0:T(1024)}, u32[]{:S(2)}) copy-start(f32[1024]{0:T(1024)} %param.19) | copy-start | bytes 12292
  74.3 10.6 %copy-start.9 = (f32[128]{0:T(128)S(1)}, f32[128]{0:T(128)}, u32[]{:S(2)}) copy-start(f32[128]{0:T(128)} %get-tuple-element.25) | copy-start | bytes 1540
  82.0 98.4 %copy-start.4 = (bf16[64,128]{1,0:T(8,128)(2,1)S(1)}, bf16[64,128]{1,0:T(8,128)(2,1)}, u32[]{:S(2)}) copy-start(bf16[64,128]{1,0:T(8,128)(2,1)} %param.23) | copy-start | bytes 49156
  84.9 91.2 %copy-start.3 = (bf16[1,128,1024]{2,1,0:T(8,128)(2,1)}, bf16[1,128,1024]{2,1,0:T(8,128)(2,1)S(1)}, u32[]{:S(2)}) copy-start(bf16[1,128,1024]{2,1,0:T(8,128)(2,1)S(1)} %fusion.11) | copy-start | bytes 786436
  84.9 98.5 %copy-start.10 = (bf16[128,64]{0,1:T(8,128)(2,1)S(1)}, bf16[128,64]{0,1:T(8,128)(2,1)}, u32[]{:S(2)}) copy-start(bf16[128,64]{0,1:T(8,128)(2,1)} %param.24) | copy-start | bytes 49156
  176.3 8.3 %copy-start.6 = (f32[16,128]{1,0:T(8,128)S(1)}, f32[16,128]{1,0:T(8,128)}, u32[]{:S(2)}) copy-start(f32[16,128]{1,0:T(8,128)} %param.25) | copy-start | bytes 24580
  180.4 5.0 %copy-start.2 = (bf16[128,8,128,1]{0,2,1,3:T(8,128)(2,1)S(1)}, bf16[128,8,128,1]{0,2,1,3:T(8,128)(2,1)}, u32[]{:S(2)}) copy-start(bf16[128,8,128,1]{0,2,1,3:T(8,128)(2,1)} %fusion.42) | copy-start | bytes 786436
  183.4 88.3 %copy-start.7 = (f32[16,128]{1,0:T(8,128)}, f32[16,128]{1,0:T(8,128)S(1)}, u32[]{:S(2)}) copy-start(f32[16,128]{1,0:T(8,128)S(1)} %get-tuple-element.22) | copy-start | bytes 24580
Sparse Core Ops, SparseCore 0:
  10.6 44.1 all-gather.2
where the time goes:
time: 279 us
  blocking collectives  171 us (61%)
  matrix products  36.1 us (13%)
  other arithmetic  34.8 us (12%)
  between operations  17.7 us (6%)
  waiting for transfers between devices  14.2 us (5%)
  local copies, waits for them, and re-layouts  4.83 us (2%)
    psum x1, blocking collectives, local(): grad_total = lax.psum(dembed_local, ('items', 'events'))  82.3 us
    psum x1, blocking collectives, local(): lax.psum((at_last(layer_out), at_last(queries), at_last(mixed), at_last(g...  51.4 us
    all_gather x1, blocking collectives, local(): lax.all_gather(user_row.astype(jnp.bfloat16), 'items', axis=0, tiled=True)  37.2 us
    convert_element_type x2, other arithmetic, dequantize(): ((nibble.astype(jnp.float32) - 7.5) * comp_scale).astype(jnp.bfloat16)  18.5 us
    all_gather x1, waiting for transfers between devices, local(): block = lax.all_gather(normed, 'events', axis=1, tiled=True)  14.1 us
    dot_general x1, matrix products, local(): jnp.dot(block.reshape(users * block_len, width), pair_weight, preferred_e...  12.6 us
    dot_general x1, matrix products, attend(): jnp.einsum('uhij,ujhd->uihd', weights, value_heads, preferred_element_typ...  7.63 us
    convert_element_type x1, other arithmetic, local(): sigmoid_linear(pair[:, :width]).astype(jnp.bfloat16)  6.85 us
  transfers between devices with their start and end apart: 1, of which 1 were waited for; matrix products, arithmetic and copies ran while one was open for 10% of the time, Pallas kernels for 0%

commit v1 on v0

v1 whole, which is shorter than its diff:
```python
import functools

import jax
import jax.numpy as jnp
from jax import lax
from jax.experimental import pallas as pl
from jax.experimental.pallas import tpu as pltpu
from jax.sharding import PartitionSpec as P

MESH = pl.DeviceIdType.MESH
HEADS = 8
COMPS = 8
ITEM_COMPS = 8
LENGTH = 2048
LANES = 128
EPS = 1e-05
F32, BF16 = jnp.float32, jnp.bfloat16
CHUNK = 512
ORDER = (4, 6, 5, 7, 2, 3, 0, 1)


def dot(a, b, ca=1, cb=0):
    return lax.dot_general(a, b, (((ca,), (cb,)), ((), ())), preferred_element_type=F32)


def silu(v):
    half = 0.5 * v
    return half * jnp.tanh(half) + half


def sigmoid(v):
    return 0.5 * jnp.tanh(0.5 * v) + 0.5


def iota(shape, dim):
    return lax.broadcasted_iota(jnp.int32, shape, dim)


def cols(h):
    return slice(h * LANES, (h + 1) * LANES)


def mean_all(v, count):
    return jnp.sum(jnp.sum(v, axis=1, keepdims=True), axis=0, keepdims=True) * (1.0 / count)


def to_rows(c):
    return jnp.concatenate([jnp.broadcast_to(c[h : h + 1, :], (8, LANES)) for h in range(8)], axis=1)


def to_compact(rows):
    sub = iota((8, LANES), 0)
    out = jnp.zeros((8, LANES), F32)
    for h in range(8):
        out = out + jnp.where(sub == h, rows[:, cols(h)], 0.0)
    return out


def kernel(
    n_items,
    n_events,
    hist_in,
    actions_ref,
    table_in,
    lengths_ref,
    igain_ref,
    igain_c_ref,
    w_in,
    ogain_ref,
    ogain_c_ref,
    wo_in,
    codes_in,
    scale_ref,
    g1_ref,
    g2t_ref,
    teacher_ref,
    layer_ref,
    scores_ref,
    dval_ref,
    hist,
    table,
    codes,
    w,
    wo,
    in_sem,
    w_sem,
    summed,
    lhs,
    gate_u,
    kv_send,
    q_send,
    kv_all,
    q_all,
    mret,
    mixbuf,
    last_src,
    last_buf,
    part_src,
    part_buf,
    user_src,
    user_buf,
    de_src,
    rs_buf,
    ar_src,
    ar_buf,
    lref,
    dref,
    items_t,
    small_send,
    small_recv,
    loc_sem,
    kv_ssem,
    kv_rsem,
    q_ssem,
    q_rsem,
    fwd_ssem,
    fwd_rsem,
    ret_ssem,
    ret_rsem,
):
    i = lax.axis_index("items")
    e = lax.axis_index("events")
    chips = n_events // 2
    my_chip, core = e // 2, e % 2
    sibling = 2 * my_chip + (1 - core)
    rows = hist.shape[0]
    width = hist.shape[1]
    length = lengths_ref[0]

    loads = [
        pltpu.make_async_copy(hist_in.at[0], hist, in_sem.at[0]),
        pltpu.make_async_copy(table_in, table, in_sem.at[1]),
        pltpu.make_async_copy(codes_in, codes, in_sem.at[2]),
        pltpu.make_async_copy(wo_in, wo, in_sem.at[3]),
    ]
    wloads = {
        c: pltpu.make_async_copy(
            w_in.at[:, pl.ds(c * CHUNK, CHUNK)], w.at[c], w_sem.at[c]
        )
        for c in ORDER
    }
    loads[0].start()
    loads[1].start()
    for c in ORDER:
        wloads[c].start()
    loads[2].start()
    loads[3].start()

    barrier = pltpu.get_barrier_semaphore()

    def greet_events(k, _):
        pl.semaphore_signal(
            barrier, inc=1, device_id=(i, lax.rem(e + k, n_events)), device_id_type=MESH
        )
        return 0

    def greet_items(k, _):
        pl.semaphore_signal(
            barrier, inc=1, device_id=(lax.rem(i + k, n_items), e), device_id_type=MESH
        )
        return 0

    lax.fori_loop(1, n_events, greet_events, 0)
    lax.fori_loop(1, n_items, greet_items, 0)

    def to_events(src, buf, phase):
        def go(k, _):
            pltpu.make_async_remote_copy(
                src_ref=src,
                dst_ref=buf.at[k - 1],
                send_sem=small_send.at[phase],
                recv_sem=small_recv.at[phase],
                device_id=(i, lax.rem(e + k, n_events)),
                device_id_type=MESH,
            ).start()
            return 0

        lax.fori_loop(1, n_events, go, 0)

    def small_wait(buf, count, sem):
        part = buf.at[pl.ds(0, count)]
        pltpu.make_async_copy(part, part, sem).wait()

    loads[0].wait()
    loads[1].wait()
    onehot_t = (iota((16, rows), 0) == jnp.broadcast_to(actions_ref[...], (16, rows))).astype(BF16)
    s_val = hist[...].astype(F32) + dot(onehot_t, table[...], 0, 0)
    summed[...] = s_val
    at_last = (iota((rows, LANES), 0) + e * rows) == (length - 1)
    picked = jnp.concatenate(
        [jnp.sum(jnp.where(at_last, s_val[:, cols(h)], 0.0), axis=0, keepdims=True) for h in range(8)],
        axis=0,
    )
    last_src[...] = picked
    center = s_val - jnp.mean(s_val, axis=1, keepdims=True)
    spread = lax.rsqrt(jnp.mean(center * center, axis=1, keepdims=True) + EPS)
    lhs[pl.ds(0, rows), :] = (center * spread * igain_ref[...]).astype(BF16)

    pl.semaphore_wait(barrier, n_events - 1 + n_items - 1)
    to_events(last_src, last_buf, 0)

    normed = lhs[pl.ds(0, rows), :]
    keep_row = (iota((rows, LANES), 0) + e * rows) < length
    for c in (4, 6, 5, 7):
        wloads[c].wait()
        y = silu(dot(normed, w[c]))
        for j in range(CHUNK // LANES):
            head = (c % 2) * (CHUNK // LANES) + j
            block = y[:, cols(j)]
            if c < 6:
                kv_send[head, 0] = block.astype(BF16)
            else:
                kv_send[head, 1] = jnp.where(keep_row, block, 0.0).astype(BF16)

    small_wait(last_buf, n_events - 1, small_recv.at[0])
    summed_c = last_src[...]
    for k in range(n_events - 1):
        summed_c = summed_c + last_buf[k]
    center = summed_c - mean_all(summed_c, width)
    spread = lax.rsqrt(mean_all(center * center, width) + EPS)
    last_rows = to_rows(center * spread * igain_c_ref[...])
    lhs[pl.ds(rows, 16), :] = jnp.concatenate([last_rows, last_rows], axis=0).astype(BF16)

    both = lhs[...]
    sub = iota((8, LANES), 0)
    q_scores = jnp.zeros((8, rows), F32)
    for c in (2, 3):
        wloads[c].wait()
        y = silu(dot(both, w[c]))
        for j in range(CHUNK // LANES):
            head = (c % 2) * (CHUNK // LANES) + j
            q_send[head] = y[:rows, cols(j)].astype(BF16)
            q_diag = jnp.where(sub == head, y[rows : rows + 8, cols(j)], 0.0).astype(BF16)
            q_scores = q_scores + dot(q_diag, kv_send[head, 0], 1, 1)

    inv = width // HEADS
    keep_col = (iota((8, rows), 1) + e * rows) < length
    w_last = jnp.where(keep_col, silu(q_scores * inv ** (-0.5)) * (1.0 / LENGTH), 0.0).astype(BF16)
    part = jnp.zeros((8, LANES), F32)
    for head in range(HEADS):
        part = part + jnp.where(sub == head, dot(w_last, kv_send[head, 1]), 0.0)
    part_src[...] = part
    to_events(part_src, part_buf, 1)

    owner = lax.rem(e + my_chip, 2)

    def kv_copy(k, target_core, block, sem_s, sem_r):
        chip = lax.rem(my_chip + k, chips)
        return pltpu.make_async_remote_copy(
            src_ref=kv_send.at[chip],
            dst_ref=kv_all.at[block],
            send_sem=sem_s,
            recv_sem=sem_r,
            device_id=(i, 2 * chip + target_core),
            device_id_type=MESH,
        )

    own_kv = pltpu.make_async_copy(kv_send.at[my_chip], kv_all.at[e], loc_sem)
    own_kv.start()
    sib_kv = pltpu.make_async_remote_copy(
        src_ref=kv_send.at[my_chip],
        dst_ref=kv_all.at[e],
        send_sem=fwd_ssem,
        recv_sem=fwd_rsem,
        device_id=(i, sibling),
        device_id_type=MESH,
    )
    sib_kv.start()

    def send_kv(k, _):
        kv_copy(k, core, e, kv_ssem, kv_rsem.at[k]).start()
        return 0

    lax.fori_loop(1, chips, send_kv, 0)

    def q_remote(chip):
        return pltpu.make_async_remote_copy(
            src_ref=q_send.at[chip],
            dst_ref=q_all.at[my_chip],
            send_sem=q_ssem,
            recv_sem=q_rsem,
            device_id=(i, 2 * chip + owner),
            device_id_type=MESH,
        )

    def send_q(k, _):
        q_remote(lax.rem(my_chip + k, chips)).start()
        return 0

    lax.fori_loop(1, chips, send_q, 0)

    @pl.when(owner == core)
    def _():
        pltpu.make_async_copy(q_send.at[my_chip], q_all.at[my_chip], q_rsem).start()

    @pl.when(owner != core)
    def _():
        q_remote(my_chip).start()

    gate_rows = []
    for c in (0, 1):
        wloads[c].wait()
        y = silu(dot(both, w[c]))
        gate_u[:, c * CHUNK : (c + 1) * CHUNK] = y[:rows]
        gate_rows.append(y[rows : rows + 8])
    gate_c = to_compact(jnp.concatenate(gate_rows, axis=1))

    loads[2].wait()
    p_i, q_i = iota((512, 512), 0), iota((512, 512), 1)
    expand = jnp.where(p_i == 4 * (q_i & 127) + (q_i >> 7), 1.0, 0.0).astype(BF16)
    for half in range(2):
        words = codes[:, cols(half)]
        nibbles = jnp.concatenate(
            [(((words >> (4 * n)) & 15).astype(F32) - 7.5).astype(BF16) for n in range(4)], axis=1
        )
        raw = dot(expand, nibbles, 1, 1)
        for j in range(4):
            c = half * 4 + j
            items_t[c] = (raw[j * LANES : (j + 1) * LANES] * scale_ref[c : c + 1, :]).astype(BF16)
    logit_count = COMPS * ITEM_COMPS
    r_i, s_i = iota((logit_count, logit_count), 0), iota((logit_count, logit_count), 1)
    perm = jnp.where(s_i == (r_i & 7) * 8 + (r_i >> 3), 1.0, 0.0).astype(BF16)
    g1, g2t = g1_ref[...], g2t_ref[...]
    m_first_t = dot(g1, perm, 0, 1).astype(BF16)
    m_first = dot(perm, g1).astype(BF16)
    m_second_t = dot(perm, g2t).astype(BF16)
    m_second = dot(g2t, perm, 0, 1).astype(BF16)

    small_wait(part_buf, n_events - 1, small_recv.at[1])
    mixed_c = part_src[...]
    for k in range(n_events - 1):
        mixed_c = mixed_c + part_buf[k]
    center_c = mixed_c - mean_all(mixed_c, width)
    spread_c = lax.rsqrt(mean_all(center_c * center_c, width) + EPS)
    normal_c = center_c * spread_c
    gated_c = normal_c * ogain_c_ref[...] * gate_c
    loads[3].wait()
    user_rows = dot(to_rows(gated_c).astype(BF16), wo[...])
    user_c = (summed_c + to_compact(user_rows)).astype(BF16).astype(F32)
    user_src[...] = user_c
    user_buf[i] = user_c

    def send_user(k, _):
        pltpu.make_async_remote_copy(
            src_ref=user_src,
            dst_ref=user_buf.at[i],
            send_sem=small_send.at[2],
            recv_sem=small_recv.at[2],
            device_id=(lax.rem(i + k, n_items), e),
            device_id_type=MESH,
        ).start()
        return 0

    lax.fori_loop(1, n_items, send_user, 0)

    users = n_items
    small_wait(user_buf, n_items - 1, small_recv.at[2])
    everyone = user_buf[...].reshape(users * 8, LANES).astype(BF16)
    for c in range(ITEM_COMPS):
        part_l = dot(everyone, items_t[c])
        for b in range(users):
            lref[c * 8 : (c + 1) * 8, cols(b)] = part_l[b * 8 : (b + 1) * 8]
    for b0 in range(0, users, 2):
        span = slice(b0 * LANES, (b0 + 2) * LANES)
        logits = lref[:, span]
        pre = dot(m_first_t, logits.astype(BF16))
        sig = sigmoid(pre)
        gates = sigmoid(dot(m_second_t, (pre * sig).astype(BF16)))
        gl = gates * logits
        score = jnp.sum(gl, axis=0, keepdims=True)
        targets = jnp.concatenate(
            [teacher_ref[b0 : b0 + 1, :], teacher_ref[b0 + 1 : b0 + 2, :]], axis=1
        )
        scores_ref[b0 : b0 + 1, :] = score[:, :LANES]
        scores_ref[b0 + 1 : b0 + 2, :] = score[:, LANES:]
        slope = (gl * (1.0 - gates)).astype(BF16)
        back = dot(m_second, slope) * (sig * (1.0 + pre * (1.0 - sig)))
        dlog = (score - targets) * (gates + dot(m_first, back.astype(BF16)))
        for c in range(ITEM_COMPS):
            for j in range(2):
                b = b0 + j
                dref[c, b * 8 : (b + 1) * 8, :] = dlog[c * 8 : (c + 1) * 8, cols(j)]
    demb = jnp.zeros((users * 8, LANES), F32)
    for c in range(ITEM_COMPS):
        demb = demb + dot(dref[c].astype(BF16), items_t[c], 1, 1)
    de_src[...] = demb.reshape(users, 8, LANES)

    def send_de(k, _):
        other = lax.rem(i + k, n_items)
        pltpu.make_async_remote_copy(
            src_ref=de_src.at[other],
            dst_ref=rs_buf.at[k - 1],
            send_sem=small_send.at[3],
            recv_sem=small_recv.at[3],
            device_id=(other, e),
            device_id_type=MESH,
        ).start()
        return 0

    lax.fori_loop(1, n_items, send_de, 0)

    own_kv.wait()

    def forward(k, _):
        source = 2 * lax.rem(my_chip + chips - k, chips) + core
        pltpu.make_async_copy(kv_all.at[source], kv_all.at[source], kv_rsem.at[k]).wait()
        pltpu.make_async_remote_copy(
            src_ref=kv_all.at[source],
            dst_ref=kv_all.at[source],
            send_sem=fwd_ssem,
            recv_sem=fwd_rsem,
            device_id=(i, sibling),
            device_id_type=MESH,
        ).start()
        return 0

    lax.fori_loop(1, chips, forward, 0)

    small_wait(rs_buf, n_items - 1, small_recv.at[3])
    red = de_src[i]
    for k in range(n_items - 1):
        red = red + rs_buf[k]
    ar_src[...] = red
    to_events(ar_src, ar_buf, 4)

    half_blocks = kv_all.at[pl.ds(0, chips)]
    pltpu.make_async_copy(half_blocks, half_blocks, fwd_rsem).wait()
    pltpu.make_async_copy(q_all, q_all, q_rsem).wait()
    half_scale = 0.5 * inv ** (-0.5)
    for n in range(chips):
        query = q_all[n]
        odd = lax.rem(core + n, 2)
        acc = jnp.zeros((rows, LANES), F32)
        for m in range(n + 1):
            key = jnp.concatenate([kv_all[2 * m, 0], kv_all[2 * m + 1, 0]], axis=0)
            value = jnp.concatenate([kv_all[2 * m, 1], kv_all[2 * m + 1, 1]], axis=0)
            half = dot(query, key, 1, 1) * half_scale
            weight = half * jnp.tanh(half) + half
            if m == n:
                causal = iota((rows, 2 * rows), 1) <= iota((rows, 2 * rows), 0) + odd * rows
                weight = jnp.where(causal, weight, 0.0)
            acc = acc + dot(weight.astype(BF16), value)
        mret[n] = acc

    def ret_remote(n, target):
        return pltpu.make_async_remote_copy(
            src_ref=mret.at[n],
            dst_ref=mixbuf.at[my_chip],
            send_sem=ret_ssem,
            recv_sem=ret_rsem,
            device_id=(i, target),
            device_id_type=MESH,
        )

    def ret_target(n):
        return 2 * n + lax.rem(n + core, 2)

    def send_ret(n, _):
        target = ret_target(n)

        @pl.when(target == e)
        def _():
            pltpu.make_async_copy(mret.at[n], mixbuf.at[my_chip], ret_rsem).start()

        @pl.when(target != e)
        def _():
            ret_remote(n, target).start()

        return 0

    lax.fori_loop(0, chips, send_ret, 0)

    small_wait(ar_buf, n_events - 1, small_recv.at[4])
    total = ar_src[...]
    for k in range(n_events - 1):
        total = total + ar_buf[k]
    dgated = to_compact(dot(to_rows(total).astype(BF16), wo[...], 1, 1))
    s_c = dgated * gate_c * ogain_c_ref[...]
    dmixed = (
        s_c - mean_all(s_c, width) - normal_c * mean_all(s_c * normal_c, width)
    ) * spread_c
    diag = jnp.concatenate([jnp.where(sub == h, dmixed, 0.0) for h in range(8)], axis=1)
    hi = diag.astype(BF16)
    lo = (diag - hi.astype(F32)).astype(BF16)
    w2 = jnp.concatenate([w_last.astype(F32), w_last.astype(F32)], axis=0).astype(BF16)
    hilo = jnp.concatenate([hi.astype(F32), lo.astype(F32)], axis=0).astype(BF16)
    dval_ref[0] = dot(w2, hilo, 0, 0)

    pltpu.make_async_copy(mixbuf, mixbuf, ret_rsem).wait()
    scale = 1.0 / LENGTH
    tot = jnp.zeros((rows, 1), F32)
    for h in range(HEADS):
        tot = tot + jnp.sum(mixbuf[h], axis=1, keepdims=True)
    mean = tot * (1.0 / width)
    var = jnp.zeros((rows, 1), F32)
    for h in range(HEADS):
        c_h = (mixbuf[h] - mean) * scale
        var = var + jnp.sum(c_h * c_h, axis=1, keepdims=True)
    spread = lax.rsqrt(var * (1.0 / width) + EPS) * scale
    gated = jnp.concatenate(
        [
            ((mixbuf[h] - mean) * spread * ogain_ref[:, cols(h)] * gate_u[:, cols(h)]).astype(BF16)
            for h in range(HEADS)
        ],
        axis=1,
    )
    layer_ref[0] = (summed[...] + dot(gated, wo[...])).astype(BF16)

    small_wait(last_buf, n_events - 1, small_send.at[0])
    small_wait(part_buf, n_events - 1, small_send.at[1])
    small_wait(user_buf, n_items - 1, small_send.at[2])
    small_wait(rs_buf, n_items - 1, small_send.at[3])
    small_wait(ar_buf, n_events - 1, small_send.at[4])
    kv_part = kv_send.at[pl.ds(0, chips - 1)]
    pltpu.make_async_copy(kv_part, kv_part, kv_ssem).wait()
    pltpu.make_async_copy(kv_send, kv_send, fwd_ssem).wait()
    q_part = q_send.at[pl.ds(0, chips - 1)]
    pltpu.make_async_copy(q_part, q_part, q_ssem).wait()

    @pl.when(owner != core)
    def _():
        q_remote(my_chip).wait_send()

    def ret_wait(n, _):
        target = ret_target(n)

        @pl.when(target != e)
        def _():
            ret_remote(n, target).wait_send()

        return 0

    lax.fori_loop(0, chips, ret_wait, 0)


def local(
    n_items,
    n_events,
    history,
    actions,
    action_table,
    lengths,
    input_gain,
    input_weight,
    output_gain,
    output_weight,
    item_codes,
    item_scale,
    gate_first,
    gate_second,
    teacher,
):
    _, rows, width = history.shape
    chips = n_events // 2
    items = item_codes.shape[0]
    users = n_items
    small = (8, LANES)
    vmem = pl.BlockSpec(memory_space=pltpu.VMEM)
    smem = pl.BlockSpec(memory_space=pltpu.SMEM)
    hbm = pl.BlockSpec(memory_space=pl.ANY)
    dma = pltpu.SemaphoreType.DMA
    layer, scores, dvalues = pl.pallas_call(
        functools.partial(kernel, n_items, n_events),
        out_shape=(
            jax.ShapeDtypeStruct((1, rows, width), BF16),
            jax.ShapeDtypeStruct((users, items), F32),
            jax.ShapeDtypeStruct((1, rows, width), F32),
        ),
        in_specs=[hbm, vmem, hbm, smem, vmem, vmem, hbm, vmem, vmem, hbm, hbm, vmem, vmem, vmem, vmem],
        out_specs=(vmem, vmem, vmem),
        scratch_shapes=[
            pltpu.VMEM((rows, width), BF16),
            pltpu.VMEM(action_table.shape, BF16),
            pltpu.VMEM(item_codes.shape, jnp.int32),
            pltpu.VMEM((4 * width // CHUNK, width, CHUNK), BF16),
            pltpu.VMEM((width, width), BF16),
            dma((4,)),
            dma((4 * width // CHUNK,)),
            pltpu.VMEM((rows, width), F32),
            pltpu.VMEM((rows + 16, width), BF16),
            pltpu.VMEM((rows, width), F32),
            pltpu.VMEM((HEADS, 2, rows, LANES), BF16),
            pltpu.VMEM((HEADS, rows, LANES), BF16),
            pltpu.VMEM((n_events, 2, rows, LANES), BF16),
            pltpu.VMEM((chips, rows, LANES), BF16),
            pltpu.VMEM((chips, rows, LANES), F32),
            pltpu.VMEM((HEADS, rows, LANES), F32),
            pltpu.VMEM(small, F32),
            pltpu.VMEM((n_events - 1,) + small, F32),
            pltpu.VMEM(small, F32),
            pltpu.VMEM((n_events - 1,) + small, F32),
            pltpu.VMEM(small, F32),
            pltpu.VMEM((n_items,) + small, F32),
            pltpu.VMEM((n_items,) + small, F32),
            pltpu.VMEM((n_items - 1,) + small, F32),
            pltpu.VMEM(small, F32),
            pltpu.VMEM((n_events - 1,) + small, F32),
            pltpu.VMEM((COMPS * ITEM_COMPS, users * LANES), F32),
            pltpu.VMEM((ITEM_COMPS, users * 8, LANES), F32),
            pltpu.VMEM((ITEM_COMPS, LANES, items), BF16),
            dma((5,)),
            dma((5,)),
            dma(()),
            dma(()),
            dma((chips,)),
            dma(()),
            dma(()),
            dma(()),
            dma(()),
            dma(()),
            dma(()),
        ],
        compiler_params=pltpu.CompilerParams(
            collective_id=0, has_side_effects=True, vmem_limit_bytes=50 * 1024 * 1024
        ),
    )(
        history,
        actions,
        action_table,
        lengths,
        input_gain.reshape(1, width),
        input_gain.reshape(8, LANES),
        input_weight,
        output_gain.reshape(1, width),
        output_gain.reshape(8, LANES),
        output_weight,
        item_codes,
        item_scale.T,
        gate_first,
        gate_second.T,
        teacher,
    )
    return layer, scores, dvalues


def solution(mesh):
    in_specs = (
        P("items", "events", None),
        P("items", "events"),
        P(),
        P("items"),
        P(),
        P(),
        P(),
        P(),
        P(("items", "events"), None),
        P(("items", "events"), None),
        P(),
        P(),
        P(None, ("items", "events")),
    )
    out_specs = (
        P("items", "events", None),
        P(None, ("items", "events")),
        P("items", "events", None),
    )
    body = functools.partial(local, mesh.shape["items"], mesh.shape["events"])
    return jax.shard_map(body, mesh=mesh, in_specs=in_specs, out_specs=out_specs, check_vma=False)
```

time: 279 us -> 66.7 us (0.24)
  blocking collectives: 171 us -> 0 us
  Pallas kernels: 0 us -> 53.8 us
  matrix products: 36.1 us -> 0 us
  other arithmetic: 34.8 us -> 0 us
  between operations: 17.7 us -> 1.31 us
  waiting for transfers between devices: 14.2 us -> 0 us
  local copies, waits for them, and re-layouts: 4.83 us -> 11.1 us
    psum x2 -> x0, blocking collectives: 134 us -> none  [the longest x1 82.3 us: local(): grad_total = lax.psum(dembed_local, ('items', 'events'))]
    pallas_call x0 -> x1, Pallas kernels: none -> 53.8 us  [local(): pl.pallas_call(functools.partial(kernel, n_items, n_events), out_shape=(j...]
    all_gather x1 -> x0, blocking collectives: 37.2 us -> none  [local(): lax.all_gather(user_row.astype(jnp.bfloat16), 'items', axis=0, tiled=True)]
    dot_general x12 -> x0, matrix products: 36.1 us -> none  [the longest x1 12.6 us: local(): jnp.dot(block.reshape(users * block_len, width), pair_weight, preferred_e...]
    convert_element_type x5 -> x0, other arithmetic: 27.4 us -> none  [the longest x2 18.5 us: dequantize(): ((nibble.astype(jnp.float32) - 7.5) * comp_scale).astype(jnp.bfloat16)]
    all_gather x1 -> x0, waiting for transfers between devices: 14.1 us -> none  [local(): block = lax.all_gather(normed, 'events', axis=1, tiled=True)]
    unnamed x26 -> x25, local copies, waits for them, and re-layouts: 3.26 us -> 11.1 us
    reduce_sum x5 -> x0, other arithmetic: 3.7 us -> none  [the longest x1 2.13 us: at_last(): return jnp.sum(pick_mask * field.astype(jnp.float32), axis=1)]
  transfers between devices with their start and end apart: 1 -> 0, of which waited for: 1 -> 0; matrix products, arithmetic and copies ran while one was open for 10% -> 0% of each run, Pallas kernels for 0% -> 0%
where the time goes in v1:
time: 66.7 us; the launch traced here: 66.2 us
  Pallas kernels  53.8 us (81%)
  local copies, waits for them, and re-layouts  11.1 us (17%)
  between operations  1.31 us (2%)
    pallas_call x1, Pallas kernels, local(): pl.pallas_call(functools.partial(kernel, n_items, n_events), out_shape=(j...  53.8 us
    unnamed x25, local copies, waits for them, and re-layouts  11.1 us

profile of v1, /device:TPU:1, one launch (start us, length us, event | category | flops | bytes accessed | tf_op | source)
XLA Modules:
  0.0 66.2 jit_solution(18428578308745364074)
XLA Ops:
  1.3 0.0 copy-start
  1.3 1.6 %copy-done = bf16[1024,1024]{1,0:T(8,128)(2,1)S(1)} copy-done((bf16[1024,1024]{1,0:T(8,128)(2,1)S(1)}, bf16[1024,1024]{1,0:T(8,128)(2,1)}, u32[]{:S(2)}) %copy-start) | copy-done | bytes 2097176
  2.9 0.0 copy-start.1
  2.9 0.9 %copy-done.1 = bf16[1,128,1024]{2,1,0:T(8,128)(2,1)S(1)} copy-done((bf16[1,128,1024]{2,1,0:T(8,128)(2,1)S(1)}, bf16[1,128,1024]{2,1,0:T(8,128)(2,1)}, u32[]{:S(2)}) %copy-start.1) | copy-done | bytes 262168
  3.8 0.0 copy-start.2
  3.8 0.9 %copy-done.2 = s32[128,256]{1,0:T(8,128)S(1)} copy-done((s32[128,256]{1,0:T(8,128)S(1)}, s32[128,256]{1,0:T(8,128)}, u32[]{:S(2)}) %copy-start.2) | copy-done | bytes 131096
  4.7 0.0 copy-start.3
  4.7 0.8 %copy-done.3 = bf16[16,1024]{1,0:T(8,128)(2,1)S(1)} copy-done((bf16[16,1024]{1,0:T(8,128)(2,1)S(1)}, bf16[16,1024]{1,0:T(8,128)(2,1)}, u32[]{:S(2)}) %copy-start.3) | copy-done | bytes 32792
  5.5 0.0 copy-start.4
  5.5 0.7 %copy-done.4 = bf16[64,128]{1,0:T(8,128)(2,1)S(1)} copy-done((bf16[64,128]{1,0:T(8,128)(2,1)S(1)}, bf16[64,128]{1,0:T(8,128)(2,1)}, u32[]{:S(2)}) %copy-start.4) | copy-done | bytes 16408
  6.2 0.0 copy-start.5
  6.2 0.7 %copy-done.5 = bf16[128,64]{0,1:T(8,128)(2,1)S(1)} copy-done((bf16[128,64]{0,1:T(8,128)(2,1)S(1)}, bf16[128,64]{0,1:T(8,128)(2,1)}, u32[]{:S(2)}) %copy-start.5) | copy-done | bytes 16408
  6.9 0.0 copy-start.6
  6.9 0.7 %copy-done.6 = f32[1024]{0:T(1024)S(1)} copy-done((f32[1024]{0:T(1024)S(1)}, f32[1024]{0:T(1024)}, u32[]{:S(2)}) %copy-start.6) | copy-done | bytes 4120
  7.6 0.0 copy-start.7
  7.6 0.7 %copy-done.7 = f32[1024]{0:T(1024)S(1)} copy-done((f32[1024]{0:T(1024)S(1)}, f32[1024]{0:T(1024)}, u32[]{:S(2)}) %copy-start.7) | copy-done | bytes 4120
  8.3 0.0 copy-start.8
  8.3 0.7 %copy-done.8 = f32[16,128]{1,0:T(8,128)S(1)} copy-done((f32[16,128]{1,0:T(8,128)S(1)}, f32[16,128]{1,0:T(8,128)}, u32[]{:S(2)}) %copy-start.8) | copy-done | bytes 8216
  9.0 0.7 %copy-done.9 = f32[128,8]{0,1:T(8,128)S(1)} copy-done((f32[128,8]{0,1:T(8,128)S(1)}, f32[128,8]{0,1:T(8,128)}, u32[]{:S(2)}) %copy-start.9) | copy-done | bytes 4120
  9.7 0.7 copy-done.10
  10.3 53.8 %shard_map.148 = (bf16[1,128,1024]{2,1,0:T(8,128)(2,1)S(1)}, f32[16,128]{1,0:T(8,128)S(1)}, f32[1,128,1024]{2,1,0:T(8,128)S(1)}) custom-call(bf16[1,128,1024]{2,1,0:T(8,128)(2,1)S(1)} %copy-done.1, s32[1,128]{1,0:T(1,128)S(1)} %copy-done.10, bf16[16,1024]{1,0:T(8,128)(2,1)S(1)} %copy-done.3, s32[1]{0:T(128)S(6)} %copy.19.lengths_ref, f32[1,1024]{1,0:T(1,128)S(1)} %bitcast.7, ...), custom_call_target="tpu_custom_call" | custom-call | tf_op jit(solution)/shard_map/pallas_call | solution.py:562
  64.1 0.7 %copy.20 = bf16[1,128,1024]{2,1,0:T(8,128)(2,1)} copy(bf16[1,128,1024]{2,1,0:T(8,128)(2,1)S(1)} %get-tuple-element.6) | data formatting | bytes 524288
  64.8 0.6 copy.21
  65.4 0.8 %copy.22 = f32[1,128,1024]{2,1,0:T(8,128)} copy(f32[1,128,1024]{2,1,0:T(8,128)S(1)} %get-tuple-element.8) | data formatting | bytes 1048576
  (2 shorter events, 0.0 us)
Async XLA Ops:
  1.3 1.6 %copy-start = (bf16[1024,1024]{1,0:T(8,128)(2,1)S(1)}, bf16[1024,1024]{1,0:T(8,128)(2,1)}, u32[]{:S(2)}) copy-start(bf16[1024,1024]{1,0:T(8,128)(2,1)} %wo_in.1) | copy-start | bytes 6291460
  2.9 0.9 %copy-start.1 = (bf16[1,128,1024]{2,1,0:T(8,128)(2,1)S(1)}, bf16[1,128,1024]{2,1,0:T(8,128)(2,1)}, u32[]{:S(2)}) copy-start(bf16[1,128,1024]{2,1,0:T(8,128)(2,1)} %hist_in.1) | copy-start | bytes 786436
  3.8 0.9 %copy-start.2 = (s32[128,256]{1,0:T(8,128)S(1)}, s32[128,256]{1,0:T(8,128)}, u32[]{:S(2)}) copy-start(s32[128,256]{1,0:T(8,128)} %codes_in.1) | copy-start | bytes 393220
  4.7 0.8 %copy-start.3 = (bf16[16,1024]{1,0:T(8,128)(2,1)S(1)}, bf16[16,1024]{1,0:T(8,128)(2,1)}, u32[]{:S(2)}) copy-start(bf16[16,1024]{1,0:T(8,128)(2,1)} %table_in.1) | copy-start | bytes 98308
  5.5 0.7 %copy-start.4 = (bf16[64,128]{1,0:T(8,128)(2,1)S(1)}, bf16[64,128]{1,0:T(8,128)(2,1)}, u32[]{:S(2)}) copy-start(bf16[64,128]{1,0:T(8,128)(2,1)} %g1_ref.1) | copy-start | bytes 49156
  6.2 0.7 %copy-start.5 = (bf16[128,64]{0,1:T(8,128)(2,1)S(1)}, bf16[128,64]{0,1:T(8,128)(2,1)}, u32[]{:S(2)}) copy-start(bf16[128,64]{0,1:T(8,128)(2,1)} %param.24) | copy-start | bytes 49156
  6.9 0.7 %copy-start.6 = (f32[1024]{0:T(1024)S(1)}, f32[1024]{0:T(1024)}, u32[]{:S(2)}) copy-start(f32[1024]{0:T(1024)} %param.17) | copy-start | bytes 12292
  7.6 0.7 %copy-start.7 = (f32[1024]{0:T(1024)S(1)}, f32[1024]{0:T(1024)}, u32[]{:S(2)}) copy-start(f32[1024]{0:T(1024)} %param.19) | copy-start | bytes 12292
  8.3 0.7 %copy-start.8 = (f32[16,128]{1,0:T(8,128)S(1)}, f32[16,128]{1,0:T(8,128)}, u32[]{:S(2)}) copy-start(f32[16,128]{1,0:T(8,128)} %teacher_ref.1) | copy-start | bytes 24580
  9.0 0.7 %copy-start.9 = (f32[128,8]{0,1:T(8,128)S(1)}, f32[128,8]{0,1:T(8,128)}, u32[]{:S(2)}) copy-start(f32[128,8]{0,1:T(8,128)} %param.22) | copy-start | bytes 12292
  9.7 0.7 copy-start.10

commit v2 on v1

--- a/solution.py
+++ b/solution.py
@@ -16,6 +16,7 @@
 EPS = 1e-05
 F32, BF16 = jnp.float32, jnp.bfloat16
 CHUNK = 512
+VMEM_LIMIT = 64 * 1000 * 1000
 ORDER = (4, 6, 5, 7, 2, 3, 0, 1)
 
 
@@ -59,29 +60,42 @@
 def kernel(
     n_items,
     n_events,
+    lengths_ref,
     hist_in,
+    actions_in,
+    table_in,
+    igain_in,
+    igain_c_in,
+    ogain_in,
+    ogain_c_in,
+    scale_in,
+    g1_in,
+    g2t_in,
+    teacher_in,
+    codes_in,
+    wo_in,
+    w_in,
+    layer_out,
+    scores_out,
+    dval_out,
+    hist,
     actions_ref,
-    table_in,
-    lengths_ref,
+    table,
     igain_ref,
     igain_c_ref,
-    w_in,
     ogain_ref,
     ogain_c_ref,
-    wo_in,
-    codes_in,
     scale_ref,
     g1_ref,
     g2t_ref,
     teacher_ref,
+    codes,
+    wo,
+    w,
     layer_ref,
     scores_ref,
     dval_ref,
-    hist,
-    table,
-    codes,
-    w,
-    wo,
+    out_sem,
     in_sem,
     w_sem,
     summed,
@@ -127,24 +141,34 @@
     width = hist.shape[1]
     length = lengths_ref[0]
 
-    loads = [
-        pltpu.make_async_copy(hist_in.at[0], hist, in_sem.at[0]),
-        pltpu.make_async_copy(table_in, table, in_sem.at[1]),
-        pltpu.make_async_copy(codes_in, codes, in_sem.at[2]),
-        pltpu.make_async_copy(wo_in, wo, in_sem.at[3]),
-    ]
+    pairs = (
+        (hist_in.at[0], hist),
+        (actions_in, actions_ref),
+        (table_in, table),
+        (igain_in, igain_ref),
+        (igain_c_in, igain_c_ref),
+        (ogain_in, ogain_ref),
+        (ogain_c_in, ogain_c_ref),
+        (scale_in, scale_ref),
+        (g1_in, g1_ref),
+        (g2t_in, g2t_ref),
+        (teacher_in, teacher_ref),
+        (codes_in, codes),
+        (wo_in, wo),
+    )
+    loads = [pltpu.make_async_copy(a, b, in_sem.at[k]) for k, (a, b) in enumerate(pairs)]
     wloads = {
         c: pltpu.make_async_copy(
             w_in.at[:, pl.ds(c * CHUNK, CHUNK)], w.at[c], w_sem.at[c]
         )
         for c in ORDER
     }
-    loads[0].start()
-    loads[1].start()
+    for k in range(5):
+        loads[k].start()
     for c in ORDER:
         wloads[c].start()
-    loads[2].start()
-    loads[3].start()
+    for k in range(5, 13):
+        loads[k].start()
 
     barrier = pltpu.get_barrier_semaphore()
 
@@ -181,8 +205,8 @@
         part = buf.at[pl.ds(0, count)]
         pltpu.make_async_copy(part, part, sem).wait()
 
-    loads[0].wait()
-    loads[1].wait()
+    for k in range(5):
+        loads[k].wait()
     onehot_t = (iota((16, rows), 0) == jnp.broadcast_to(actions_ref[...], (16, rows))).astype(BF16)
     s_val = hist[...].astype(F32) + dot(onehot_t, table[...], 0, 0)
     summed[...] = s_val
@@ -305,7 +329,8 @@
         gate_rows.append(y[rows : rows + 8])
     gate_c = to_compact(jnp.concatenate(gate_rows, axis=1))
 
-    loads[2].wait()
+    for k in range(5, 12):
+        loads[k].wait()
     p_i, q_i = iota((512, 512), 0), iota((512, 512), 1)
     expand = jnp.where(p_i == 4 * (q_i & 127) + (q_i >> 7), 1.0, 0.0).astype(BF16)
     for half in range(2):
@@ -334,7 +359,7 @@
     spread_c = lax.rsqrt(mean_all(center_c * center_c, width) + EPS)
     normal_c = center_c * spread_c
     gated_c = normal_c * ogain_c_ref[...] * gate_c
-    loads[3].wait()
+    loads[12].wait()
     user_rows = dot(to_rows(gated_c).astype(BF16), wo[...])
     user_c = (summed_c + to_compact(user_rows)).astype(BF16).astype(F32)
     user_src[...] = user_c
@@ -399,6 +424,9 @@
 
     lax.fori_loop(1, n_items, send_de, 0)
 
+    out_scores = pltpu.make_async_copy(scores_ref, scores_out, out_sem.at[1])
+    out_scores.start()
+
     own_kv.wait()
 
     def forward(k, _):
@@ -484,7 +512,10 @@
     lo = (diag - hi.astype(F32)).astype(BF16)
     w2 = jnp.concatenate([w_last.astype(F32), w_last.astype(F32)], axis=0).astype(BF16)
     hilo = jnp.concatenate([hi.astype(F32), lo.astype(F32)], axis=0).astype(BF16)
-    dval_ref[0] = dot(w2, hilo, 0, 0)
+    dval_ref[...] = dot(w2, hilo, 0, 0)
+
+    out_dval = pltpu.make_async_copy(dval_ref, dval_out.at[0], out_sem.at[2])
+    out_dval.start()
 
     pltpu.make_async_copy(mixbuf, mixbuf, ret_rsem).wait()
     scale = 1.0 / LENGTH
@@ -504,7 +535,10 @@
         ],
         axis=1,
     )
-    layer_ref[0] = (summed[...] + dot(gated, wo[...])).astype(BF16)
+    layer_ref[...] = (summed[...] + dot(gated, wo[...])).astype(BF16)
+
+    out_layer = pltpu.make_async_copy(layer_ref, layer_out.at[0], out_sem.at[0])
+    out_layer.start()
 
     small_wait(last_buf, n_events - 1, small_send.at[0])
     small_wait(part_buf, n_events - 1, small_send.at[1])
@@ -531,6 +565,9 @@
         return 0
 
     lax.fori_loop(0, chips, ret_wait, 0)
+    out_scores.wait()
+    out_dval.wait()
+    out_layer.wait()
 
 
 def local(
@@ -555,7 +592,6 @@
     items = item_codes.shape[0]
     users = n_items
     small = (8, LANES)
-    vmem = pl.BlockSpec(memory_space=pltpu.VMEM)
     smem = pl.BlockSpec(memory_space=pltpu.SMEM)
     hbm = pl.BlockSpec(memory_space=pl.ANY)
     dma = pltpu.SemaphoreType.DMA
@@ -566,15 +602,28 @@
             jax.ShapeDtypeStruct((users, items), F32),
             jax.ShapeDtypeStruct((1, rows, width), F32),
         ),
-        in_specs=[hbm, vmem, hbm, smem, vmem, vmem, hbm, vmem, vmem, hbm, hbm, vmem, vmem, vmem, vmem],
-        out_specs=(vmem, vmem, vmem),
+        in_specs=[smem] + [hbm] * 14,
+        out_specs=(hbm, hbm, hbm),
         scratch_shapes=[
             pltpu.VMEM((rows, width), BF16),
+            pltpu.VMEM(actions.shape, jnp.int32),
             pltpu.VMEM(action_table.shape, BF16),
+            pltpu.VMEM((1, width), F32),
+            pltpu.VMEM((8, LANES), F32),
+            pltpu.VMEM((1, width), F32),
+            pltpu.VMEM((8, LANES), F32),
+            pltpu.VMEM((ITEM_COMPS, items), F32),
+            pltpu.VMEM(gate_first.shape, BF16),
+            pltpu.VMEM(gate_first.shape, BF16),
+            pltpu.VMEM((users, items), F32),
             pltpu.VMEM(item_codes.shape, jnp.int32),
+            pltpu.VMEM((width, width), BF16),
             pltpu.VMEM((4 * width // CHUNK, width, CHUNK), BF16),
-            pltpu.VMEM((width, width), BF16),
-            dma((4,)),
+            pltpu.VMEM((rows, width), BF16),
+            pltpu.VMEM((users, items), F32),
+            pltpu.VMEM((rows, width), F32),
+            dma((3,)),
+            dma((13,)),
             dma((4 * width // CHUNK,)),
             pltpu.VMEM((rows, width), F32),
             pltpu.VMEM((rows + 16, width), BF16),
@@ -611,26 +660,55 @@
             dma(()),
         ],
         compiler_params=pltpu.CompilerParams(
-            collective_id=0, has_side_effects=True, vmem_limit_bytes=50 * 1024 * 1024
+            collective_id=0, has_side_effects=True, vmem_limit_bytes=VMEM_LIMIT
         ),
     )(
+        lengths,
         history,
         actions,
         action_table,
-        lengths,
         input_gain.reshape(1, width),
         input_gain.reshape(8, LANES),
-        input_weight,
         output_gain.reshape(1, width),
         output_gain.reshape(8, LANES),
-        output_weight,
-        item_codes,
         item_scale.T,
         gate_first,
         gate_second.T,
         teacher,
+        item_codes,
+        output_weight,
+        input_weight,
     )
-    return layer, scores, dvalues
+    return pl.pallas_call(
+        write_out,
+        out_shape=(
+            jax.ShapeDtypeStruct((1, rows, width), BF16),
+            jax.ShapeDtypeStruct((users, items), F32),
+            jax.ShapeDtypeStruct((1, rows, width), F32),
+        ),
+        in_specs=[pl.BlockSpec(memory_space=pl.ANY)] * 3,
+        out_specs=(hbm, hbm, hbm),
+        scratch_shapes=[
+            pltpu.VMEM((1, rows, width), BF16),
+            pltpu.VMEM((users, items), F32),
+            pltpu.VMEM((1, rows, width), F32),
+            dma((2, 3)),
+        ],
+        compiler_params=pltpu.CompilerParams(vmem_limit_bytes=VMEM_LIMIT),
+    )(layer, scores, dvalues)
+
+
+def write_out(layer_in, scores_in, dval_in, layer_out, scores_out, dval_out, layer, scores, dval, sem):
+    trips = ((dval_in, dval, dval_out), (layer_in, layer, layer_out), (scores_in, scores, scores_out))
+    reads = [pltpu.make_async_copy(a, b, sem.at[0, k]) for k, (a, b, _) in enumerate(trips)]
+    writes = [pltpu.make_async_copy(b, c, sem.at[1, k]) for k, (_, b, c) in enumerate(trips)]
+    for copy in reads:
+        copy.start()
+    for first, second in zip(reads, writes):
+        first.wait()
+        second.start()
+    for copy in writes:
+        copy.wait()
 
 
 def solution(mesh):

time: 66.7 us -> 57.7 us (0.87)
  local copies, waits for them, and re-layouts: 11.1 us -> 0 us
  Pallas kernels: 53.8 us -> 56.3 us
    unnamed x25 -> x0, local copies, waits for them, and re-layouts: 11.1 us -> none
    pallas_call x0 -> x1, Pallas kernels: none -> 1.97 us  [local(): pl.pallas_call(write_out, out_shape=(jax.ShapeDtypeStruct((1, rows, width...]
where the time goes in v2:
time: 57.7 us; the launch traced here: 57.6 us
  Pallas kernels  56.3 us (98%)
  between operations  1.29 us (2%)
    pallas_call x1, Pallas kernels, local(): pl.pallas_call(functools.partial(kernel, n_items, n_events), out_shape=(j...  54.3 us
    pallas_call x1, Pallas kernels, local(): pl.pallas_call(write_out, out_shape=(jax.ShapeDtypeStruct((1, rows, width...  1.97 us

profile of v2, /device:TPU:1, one launch (start us, length us, event | category | flops | bytes accessed | tf_op | source)
XLA Modules:
  0.0 57.6 jit_solution(1933532334092825336)
XLA Ops:
  1.3 54.3 %shard_map.148 = (bf16[1,128,1024]{2,1,0:T(8,128)(2,1)}, f32[16,128]{1,0:T(8,128)}, f32[1,128,1024]{2,1,0:T(8,128)}) custom-call(s32[1]{0:T(128)S(6)} %copy.16.lengths_ref, bf16[1,128,1024]{2,1,0:T(8,128)(2,1)} %hist_in.1, s32[1,128]{1,0:T(1,128)} %actions_in.1, bf16[16,1024]{1,0:T(8,128)(2,1)} %table_in.1, f32[1,1024]{1,0:T(1,128)} %bitcast.7, ...), custom_call_target="tpu_custom_call" | custom-call | tf_op jit(solution)/shard_map/pallas_call | solution.py:598
  55.6 2.0 %shard_map.149 = (bf16[1,128,1024]{2,1,0:T(8,128)(2,1)}, f32[16,128]{1,0:T(8,128)}, f32[1,128,1024]{2,1,0:T(8,128)}) custom-call(bf16[1,128,1024]{2,1,0:T(8,128)(2,1)} %get-tuple-element.6.layer_in, f32[16,128]{1,0:T(8,128)} %get-tuple-element.7.scores_in, f32[1,128,1024]{2,1,0:T(8,128)} %get-tuple-element.8.dval_in), custom_call_target="tpu_custom_call" | custom-call | tf_op jit(solution)/shard_map/pallas_call | solution.py:682

commit v3 on v2

--- a/solution.py
+++ b/solution.py
@@ -163,12 +163,11 @@
         )
         for c in ORDER
     }
-    for k in range(5):
+    for k in range(12):
         loads[k].start()
     for c in ORDER:
         wloads[c].start()
-    for k in range(5, 13):
-        loads[k].start()
+    loads[12].start()
 
     barrier = pltpu.get_barrier_semaphore()
 
@@ -222,112 +221,6 @@
 
     pl.semaphore_wait(barrier, n_events - 1 + n_items - 1)
     to_events(last_src, last_buf, 0)
-
-    normed = lhs[pl.ds(0, rows), :]
-    keep_row = (iota((rows, LANES), 0) + e * rows) < length
-    for c in (4, 6, 5, 7):
-        wloads[c].wait()
-        y = silu(dot(normed, w[c]))
-        for j in range(CHUNK // LANES):
-            head = (c % 2) * (CHUNK // LANES) + j
-            block = y[:, cols(j)]
-            if c < 6:
-                kv_send[head, 0] = block.astype(BF16)
-            else:
-                kv_send[head, 1] = jnp.where(keep_row, block, 0.0).astype(BF16)
-
-    small_wait(last_buf, n_events - 1, small_recv.at[0])
-    summed_c = last_src[...]
-    for k in range(n_events - 1):
-        summed_c = summed_c + last_buf[k]
-    center = summed_c - mean_all(summed_c, width)
-    spread = lax.rsqrt(mean_all(center * center, width) + EPS)
-    last_rows = to_rows(center * spread * igain_c_ref[...])
-    lhs[pl.ds(rows, 16), :] = jnp.concatenate([last_rows, last_rows], axis=0).astype(BF16)
-
-    both = lhs[...]
-    sub = iota((8, LANES), 0)
-    q_scores = jnp.zeros((8, rows), F32)
-    for c in (2, 3):
-        wloads[c].wait()
-        y = silu(dot(both, w[c]))
-        for j in range(CHUNK // LANES):
-            head = (c % 2) * (CHUNK // LANES) + j
-            q_send[head] = y[:rows, cols(j)].astype(BF16)
-            q_diag = jnp.where(sub == head, y[rows : rows + 8, cols(j)], 0.0).astype(BF16)
-            q_scores = q_scores + dot(q_diag, kv_send[head, 0], 1, 1)
-
-    inv = width // HEADS
-    keep_col = (iota((8, rows), 1) + e * rows) < length
-    w_last = jnp.where(keep_col, silu(q_scores * inv ** (-0.5)) * (1.0 / LENGTH), 0.0).astype(BF16)
-    part = jnp.zeros((8, LANES), F32)
-    for head in range(HEADS):
-        part = part + jnp.where(sub == head, dot(w_last, kv_send[head, 1]), 0.0)
-    part_src[...] = part
-    to_events(part_src, part_buf, 1)
-
-    owner = lax.rem(e + my_chip, 2)
-
-    def kv_copy(k, target_core, block, sem_s, sem_r):
-        chip = lax.rem(my_chip + k, chips)
-        return pltpu.make_async_remote_copy(
-            src_ref=kv_send.at[chip],
-            dst_ref=kv_all.at[block],
-            send_sem=sem_s,
-            recv_sem=sem_r,
-            device_id=(i, 2 * chip + target_core),
-            device_id_type=MESH,
-        )
-
-    own_kv = pltpu.make_async_copy(kv_send.at[my_chip], kv_all.at[e], loc_sem)
-    own_kv.start()
-    sib_kv = pltpu.make_async_remote_copy(
-        src_ref=kv_send.at[my_chip],
-        dst_ref=kv_all.at[e],
-        send_sem=fwd_ssem,
-        recv_sem=fwd_rsem,
-        device_id=(i, sibling),
-        device_id_type=MESH,
-    )
-    sib_kv.start()
-
-    def send_kv(k, _):
-        kv_copy(k, core, e, kv_ssem, kv_rsem.at[k]).start()
-        return 0
-
-    lax.fori_loop(1, chips, send_kv, 0)
-
-    def q_remote(chip):
-        return pltpu.make_async_remote_copy(
-            src_ref=q_send.at[chip],
-            dst_ref=q_all.at[my_chip],
-            send_sem=q_ssem,
-            recv_sem=q_rsem,
-            device_id=(i, 2 * chip + owner),
-            device_id_type=MESH,
-        )
-
-    def send_q(k, _):
-        q_remote(lax.rem(my_chip + k, chips)).start()
-        return 0
-
-    lax.fori_loop(1, chips, send_q, 0)
-
-    @pl.when(owner == core)
-    def _():
-        pltpu.make_async_copy(q_send.at[my_chip], q_all.at[my_chip], q_rsem).start()
-
-    @pl.when(owner != core)
-    def _():
-        q_remote(my_chip).start()
-
-    gate_rows = []
-    for c in (0, 1):
-        wloads[c].wait()
-        y = silu(dot(both, w[c]))
-        gate_u[:, c * CHUNK : (c + 1) * CHUNK] = y[:rows]
-        gate_rows.append(y[rows : rows + 8])
-    gate_c = to_compact(jnp.concatenate(gate_rows, axis=1))
 
     for k in range(5, 12):
         loads[k].wait()
@@ -351,6 +244,57 @@
     m_second_t = dot(perm, g2t).astype(BF16)
     m_second = dot(g2t, perm, 0, 1).astype(BF16)
 
+    normed = lhs[pl.ds(0, rows), :]
+    keep_row = (iota((rows, LANES), 0) + e * rows) < length
+    for c in (4, 6, 5, 7):
+        wloads[c].wait()
+        y = silu(dot(normed, w[c]))
+        for j in range(CHUNK // LANES):
+            head = (c % 2) * (CHUNK // LANES) + j
+            block = y[:, cols(j)]
+            if c < 6:
+                kv_send[head, 0] = block.astype(BF16)
+            else:
+                kv_send[head, 1] = jnp.where(keep_row, block, 0.0).astype(BF16)
+
+    small_wait(last_buf, n_events - 1, small_recv.at[0])
+    summed_c = last_src[...]
+    for k in range(n_events - 1):
+        summed_c = summed_c + last_buf[k]
+    center = summed_c - mean_all(summed_c, width)
+    spread = lax.rsqrt(mean_all(center * center, width) + EPS)
+    last_rows = to_rows(center * spread * igain_c_ref[...])
+    lhs[pl.ds(rows, 16), :] = jnp.concatenate([last_rows, last_rows], axis=0).astype(BF16)
+
+    both = lhs[...]
+    sub = iota((8, LANES), 0)
+    q_scores = jnp.zeros((8, rows), F32)
+    for c in (2, 3):
+        wloads[c].wait()
+        y = silu(dot(both, w[c]))
+        for j in range(CHUNK // LANES):
+            head = (c % 2) * (CHUNK // LANES) + j
+            q_send[head] = y[:rows, cols(j)].astype(BF16)
+            q_diag = jnp.where(sub == head, y[rows : rows + 8, cols(j)], 0.0).astype(BF16)
+            q_scores = q_scores + dot(q_diag, kv_send[head, 0], 1, 1)
+
+    inv = width // HEADS
+    keep_col = (iota((8, rows), 1) + e * rows) < length
+    w_last = jnp.where(keep_col, silu(q_scores * inv ** (-0.5)) * (1.0 / LENGTH), 0.0).astype(BF16)
+    part = jnp.zeros((8, LANES), F32)
+    for head in range(HEADS):
+        part = part + jnp.where(sub == head, dot(w_last, kv_send[head, 1]), 0.0)
+    part_src[...] = part
+    to_events(part_src, part_buf, 1)
+
+    gate_rows = []
+    for c in (0, 1):
+        wloads[c].wait()
+        y = silu(dot(both, w[c]))
+        gate_u[:, c * CHUNK : (c + 1) * CHUNK] = y[:rows]
+        gate_rows.append(y[rows : rows + 8])
+    gate_c = to_compact(jnp.concatenate(gate_rows, axis=1))
+
     small_wait(part_buf, n_events - 1, small_recv.at[1])
     mixed_c = part_src[...]
     for k in range(n_events - 1):
@@ -377,6 +321,61 @@
         return 0
 
     lax.fori_loop(1, n_items, send_user, 0)
+
+    owner = lax.rem(e + my_chip, 2)
+
+    def kv_copy(k, target_core, block, sem_s, sem_r):
+        chip = lax.rem(my_chip + k, chips)
+        return pltpu.make_async_remote_copy(
+            src_ref=kv_send.at[chip],
+            dst_ref=kv_all.at[block],
+            send_sem=sem_s,
+            recv_sem=sem_r,
+            device_id=(i, 2 * chip + target_core),
+            device_id_type=MESH,
+        )
+
+    own_kv = pltpu.make_async_copy(kv_send.at[my_chip], kv_all.at[e], loc_sem)
+    own_kv.start()
+    sib_kv = pltpu.make_async_remote_copy(
+        src_ref=kv_send.at[my_chip],
+        dst_ref=kv_all.at[e],
+        send_sem=fwd_ssem,
+        recv_sem=fwd_rsem,
+        device_id=(i, sibling),
+        device_id_type=MESH,
+    )
+    sib_kv.start()
+
+    def send_kv(k, _):
+        kv_copy(k, core, e, kv_ssem, kv_rsem.at[k]).start()
+        return 0
+
+    lax.fori_loop(1, chips, send_kv, 0)
+
+    def q_remote(chip):
+        return pltpu.make_async_remote_copy(
+            src_ref=q_send.at[chip],
+            dst_ref=q_all.at[my_chip],
+            send_sem=q_ssem,
+            recv_sem=q_rsem,
+            device_id=(i, 2 * chip + owner),
+            device_id_type=MESH,
+        )
+
+    def send_q(k, _):
+        q_remote(lax.rem(my_chip + k, chips)).start()
+        return 0
+
+    lax.fori_loop(1, chips, send_q, 0)
+
+    @pl.when(owner == core)
+    def _():
+        pltpu.make_async_copy(q_send.at[my_chip], q_all.at[my_chip], q_rsem).start()
+
+    @pl.when(owner != core)
+    def _():
+        q_remote(my_chip).start()
 
     users = n_items
     small_wait(user_buf, n_items - 1, small_recv.at[2])
@@ -468,7 +467,7 @@
                 causal = iota((rows, 2 * rows), 1) <= iota((rows, 2 * rows), 0) + odd * rows
                 weight = jnp.where(causal, weight, 0.0)
             acc = acc + dot(weight.astype(BF16), value)
-        mret[n] = acc
+        mret[n] = acc.astype(BF16)
 
     def ret_remote(n, target):
         return pltpu.make_async_remote_copy(
@@ -521,16 +520,16 @@
     scale = 1.0 / LENGTH
     tot = jnp.zeros((rows, 1), F32)
     for h in range(HEADS):
-        tot = tot + jnp.sum(mixbuf[h], axis=1, keepdims=True)
+        tot = tot + jnp.sum(mixbuf[h].astype(F32), axis=1, keepdims=True)
     mean = tot * (1.0 / width)
     var = jnp.zeros((rows, 1), F32)
     for h in range(HEADS):
-        c_h = (mixbuf[h] - mean) * scale
+        c_h = (mixbuf[h].astype(F32) - mean) * scale
         var = var + jnp.sum(c_h * c_h, axis=1, keepdims=True)
     spread = lax.rsqrt(var * (1.0 / width) + EPS) * scale
     gated = jnp.concatenate(
         [
-            ((mixbuf[h] - mean) * spread * ogain_ref[:, cols(h)] * gate_u[:, cols(h)]).astype(BF16)
+            ((mixbuf[h].astype(F32) - mean) * spread * ogain_ref[:, cols(h)] * gate_u[:, cols(h)]).astype(BF16)
             for h in range(HEADS)
         ],
         axis=1,
@@ -632,8 +631,8 @@
             pltpu.VMEM((HEADS, rows, LANES), BF16),
             pltpu.VMEM((n_events, 2, rows, LANES), BF16),
             pltpu.VMEM((chips, rows, LANES), BF16),
-            pltpu.VMEM((chips, rows, LANES), F32),
-            pltpu.VMEM((HEADS, rows, LANES), F32),
+            pltpu.VMEM((chips, rows, LANES), BF16),
+            pltpu.VMEM((HEADS, rows, LANES), BF16),
             pltpu.VMEM(small, F32),
             pltpu.VMEM((n_events - 1,) + small, F32),
             pltpu.VMEM(small, F32),

time: 57.7 us -> 50.6 us (0.88)
  the two profiles are of different devices: /device:TPU:1 before, /device:TPU:2 now
where the time goes in v3:
time: 50.6 us; the launch traced here: 50.5 us
  Pallas kernels  49.2 us (97%)
  between operations  1.29 us (3%)
    pallas_call x1, Pallas kernels, local(): pl.pallas_call(functools.partial(kernel, n_items, n_events), out_shape=(j...  47.2 us
    pallas_call x1, Pallas kernels, local(): pl.pallas_call(write_out, out_shape=(jax.ShapeDtypeStruct((1, rows, width...  1.97 us

profile of v3, /device:TPU:2, one launch (start us, length us, event | category | flops | bytes accessed | tf_op | source)
XLA Modules:
  0.0 50.5 jit_solution(18277037968941854986)
XLA Ops:
  1.3 47.2 %shard_map.148 = (bf16[1,128,1024]{2,1,0:T(8,128)(2,1)}, f32[16,128]{1,0:T(8,128)}, f32[1,128,1024]{2,1,0:T(8,128)}) custom-call(s32[1]{0:T(128)S(6)} %copy.16.lengths_ref, bf16[1,128,1024]{2,1,0:T(8,128)(2,1)} %hist_in.1, s32[1,128]{1,0:T(1,128)} %actions_in.1, bf16[16,1024]{1,0:T(8,128)(2,1)} %table_in.1, f32[1,1024]{1,0:T(1,128)} %bitcast.7, ...), custom_call_target="tpu_custom_call" | custom-call | tf_op jit(solution)/shard_map/pallas_call | solution.py:597
  48.5 2.0 %shard_map.149 = (bf16[1,128,1024]{2,1,0:T(8,128)(2,1)}, f32[16,128]{1,0:T(8,128)}, f32[1,128,1024]{2,1,0:T(8,128)}) custom-call(bf16[1,128,1024]{2,1,0:T(8,128)(2,1)} %get-tuple-element.6.layer_in, f32[16,128]{1,0:T(8,128)} %get-tuple-element.7.scores_in, f32[1,128,1024]{2,1,0:T(8,128)} %get-tuple-element.8.dval_in), custom_call_target="tpu_custom_call" | custom-call | tf_op jit(solution)/shard_map/pallas_call | solution.py:681

commit v4 on v3

--- a/solution.py
+++ b/solution.py
@@ -16,6 +16,7 @@
 EPS = 1e-05
 F32, BF16 = jnp.float32, jnp.bfloat16
 CHUNK = 512
+GROUP = 16
 VMEM_LIMIT = 64 * 1000 * 1000
 ORDER = (4, 6, 5, 7, 2, 3, 0, 1)
 
@@ -120,6 +121,7 @@
     lref,
     dref,
     items_t,
+    items_n,
     small_send,
     small_recv,
     loc_sem,
@@ -234,7 +236,9 @@
         raw = dot(expand, nibbles, 1, 1)
         for j in range(4):
             c = half * 4 + j
-            items_t[c] = (raw[j * LANES : (j + 1) * LANES] * scale_ref[c : c + 1, :]).astype(BF16)
+            vector = raw[j * LANES : (j + 1) * LANES] * scale_ref[c : c + 1, :]
+            items_t[:, cols(c)] = vector.astype(BF16)
+            items_n[c * LANES : (c + 1) * LANES, :] = vector.T.astype(BF16)
     logit_count = COMPS * ITEM_COMPS
     r_i, s_i = iota((logit_count, logit_count), 0), iota((logit_count, logit_count), 1)
     perm = jnp.where(s_i == (r_i & 7) * 8 + (r_i >> 3), 1.0, 0.0).astype(BF16)
@@ -256,6 +260,38 @@
                 kv_send[head, 0] = block.astype(BF16)
             else:
                 kv_send[head, 1] = jnp.where(keep_row, block, 0.0).astype(BF16)
+
+    owner = lax.rem(e + my_chip, 2)
+
+    def kv_copy(k, target_core, block, sem_s, sem_r):
+        chip = lax.rem(my_chip + k, chips)
+        return pltpu.make_async_remote_copy(
+            src_ref=kv_send.at[chip],
+            dst_ref=kv_all.at[block],
+            send_sem=sem_s,
+            recv_sem=sem_r,
+            device_id=(i, 2 * chip + target_core),
+            device_id_type=MESH,
+        )
+
+    own_kv = pltpu.make_async_copy(kv_send.at[my_chip], kv_all.at[e], loc_sem)
+    own_kv.start()
+    sib_kv = pltpu.make_async_remote_copy(
+        src_ref=kv_send.at[my_chip],
+        dst_ref=kv_all.at[e],
+        send_sem=fwd_ssem,
+        recv_sem=fwd_rsem,
+        device_id=(i, sibling),
+        device_id_type=MESH,
+    )
+    sib_kv.start()
+
+    def send_kv(k, _):
+        kv_copy(k, core, e, kv_ssem, kv_rsem.at[k]).start()
+        return 0
+
+    lax.fori_loop(1, chips, send_kv, 0)
+
 
     small_wait(last_buf, n_events - 1, small_recv.at[0])
     summed_c = last_src[...]
@@ -322,37 +358,6 @@
 
     lax.fori_loop(1, n_items, send_user, 0)
 
-    owner = lax.rem(e + my_chip, 2)
-
-    def kv_copy(k, target_core, block, sem_s, sem_r):
-        chip = lax.rem(my_chip + k, chips)
-        return pltpu.make_async_remote_copy(
-            src_ref=kv_send.at[chip],
-            dst_ref=kv_all.at[block],
-            send_sem=sem_s,
-            recv_sem=sem_r,
-            device_id=(i, 2 * chip + target_core),
-            device_id_type=MESH,
-        )
-
-    own_kv = pltpu.make_async_copy(kv_send.at[my_chip], kv_all.at[e], loc_sem)
-    own_kv.start()
-    sib_kv = pltpu.make_async_remote_copy(
-        src_ref=kv_send.at[my_chip],
-        dst_ref=kv_all.at[e],
-        send_sem=fwd_ssem,
-        recv_sem=fwd_rsem,
-        device_id=(i, sibling),
-        device_id_type=MESH,
-    )
-    sib_kv.start()
-
-    def send_kv(k, _):
-        kv_copy(k, core, e, kv_ssem, kv_rsem.at[k]).start()
-        return 0
-
-    lax.fori_loop(1, chips, send_kv, 0)
-
     def q_remote(chip):
         return pltpu.make_async_remote_copy(
             src_ref=q_send.at[chip],
@@ -376,55 +381,6 @@
     @pl.when(owner != core)
     def _():
         q_remote(my_chip).start()
-
-    users = n_items
-    small_wait(user_buf, n_items - 1, small_recv.at[2])
-    everyone = user_buf[...].reshape(users * 8, LANES).astype(BF16)
-    for c in range(ITEM_COMPS):
-        part_l = dot(everyone, items_t[c])
-        for b in range(users):
-            lref[c * 8 : (c + 1) * 8, cols(b)] = part_l[b * 8 : (b + 1) * 8]
-    for b0 in range(0, users, 2):
-        span = slice(b0 * LANES, (b0 + 2) * LANES)
-        logits = lref[:, span]
-        pre = dot(m_first_t, logits.astype(BF16))
-        sig = sigmoid(pre)
-        gates = sigmoid(dot(m_second_t, (pre * sig).astype(BF16)))
-        gl = gates * logits
-        score = jnp.sum(gl, axis=0, keepdims=True)
-        targets = jnp.concatenate(
-            [teacher_ref[b0 : b0 + 1, :], teacher_ref[b0 + 1 : b0 + 2, :]], axis=1
-        )
-        scores_ref[b0 : b0 + 1, :] = score[:, :LANES]
-        scores_ref[b0 + 1 : b0 + 2, :] = score[:, LANES:]
-        slope = (gl * (1.0 - gates)).astype(BF16)
-        back = dot(m_second, slope) * (sig * (1.0 + pre * (1.0 - sig)))
-        dlog = (score - targets) * (gates + dot(m_first, back.astype(BF16)))
-        for c in range(ITEM_COMPS):
-            for j in range(2):
-                b = b0 + j
-                dref[c, b * 8 : (b + 1) * 8, :] = dlog[c * 8 : (c + 1) * 8, cols(j)]
-    demb = jnp.zeros((users * 8, LANES), F32)
-    for c in range(ITEM_COMPS):
-        demb = demb + dot(dref[c].astype(BF16), items_t[c], 1, 1)
-    de_src[...] = demb.reshape(users, 8, LANES)
-
-    def send_de(k, _):
-        other = lax.rem(i + k, n_items)
-        pltpu.make_async_remote_copy(
-            src_ref=de_src.at[other],
-            dst_ref=rs_buf.at[k - 1],
-            send_sem=small_send.at[3],
-            recv_sem=small_recv.at[3],
-            device_id=(other, e),
-            device_id_type=MESH,
-        ).start()
-        return 0
-
-    lax.fori_loop(1, n_items, send_de, 0)
-
-    out_scores = pltpu.make_async_copy(scores_ref, scores_out, out_sem.at[1])
-    out_scores.start()
 
     own_kv.wait()
 
@@ -443,12 +399,49 @@
 
     lax.fori_loop(1, chips, forward, 0)
 
-    small_wait(rs_buf, n_items - 1, small_recv.at[3])
-    red = de_src[i]
-    for k in range(n_items - 1):
-        red = red + rs_buf[k]
-    ar_src[...] = red
-    to_events(ar_src, ar_buf, 4)
+
+    users = n_items
+    small_wait(user_buf, n_items - 1, small_recv.at[2])
+    everyone = user_buf[...].reshape(users * 8, LANES).astype(BF16)
+    part_l = dot(everyone, items_t[...])
+    for c in range(ITEM_COMPS):
+        for b in range(users):
+            lref[c * 8 : (c + 1) * 8, cols(b)] = part_l[b * 8 : (b + 1) * 8, cols(c)]
+    for b0 in range(0, users, GROUP):
+        logits = lref[:, b0 * LANES : (b0 + GROUP) * LANES]
+        pre = dot(m_first_t, logits.astype(BF16))
+        sig = sigmoid(pre)
+        gates = sigmoid(dot(m_second_t, (pre * sig).astype(BF16)))
+        gl = gates * logits
+        score = jnp.sum(gl, axis=0, keepdims=True)
+        targets = jnp.concatenate([teacher_ref[b0 + j : b0 + j + 1, :] for j in range(GROUP)], axis=1)
+        slope = (gl * (1.0 - gates)).astype(BF16)
+        back = dot(m_second, slope) * (sig * (1.0 + pre * (1.0 - sig)))
+        dlog = (score - targets) * (gates + dot(m_first, back.astype(BF16)))
+        for j in range(GROUP):
+            b = b0 + j
+            scores_ref[b : b + 1, :] = score[:, cols(j)]
+            for c in range(ITEM_COMPS):
+                dref[b * 8 : (b + 1) * 8, cols(c)] = dlog[c * 8 : (c + 1) * 8, cols(j)]
+    demb = dot(dref[...].astype(BF16), items_n[...])
+    de_src[...] = demb.reshape(users, 8, LANES)
+
+    def send_de(k, _):
+        other = lax.rem(i + k, n_items)
+        pltpu.make_async_remote_copy(
+            src_ref=de_src.at[other],
+            dst_ref=rs_buf.at[k - 1],
+            send_sem=small_send.at[3],
+            recv_sem=small_recv.at[3],
+            device_id=(other, e),
+            device_id_type=MESH,
+        ).start()
+        return 0
+
+    lax.fori_loop(1, n_items, send_de, 0)
+
+    out_scores = pltpu.make_async_copy(scores_ref, scores_out, out_sem.at[1])
+    out_scores.start()
 
     half_blocks = kv_all.at[pl.ds(0, chips)]
     pltpu.make_async_copy(half_blocks, half_blocks, fwd_rsem).wait()
@@ -497,24 +490,12 @@
 
     lax.fori_loop(0, chips, send_ret, 0)
 
-    small_wait(ar_buf, n_events - 1, small_recv.at[4])
-    total = ar_src[...]
-    for k in range(n_events - 1):
-        total = total + ar_buf[k]
-    dgated = to_compact(dot(to_rows(total).astype(BF16), wo[...], 1, 1))
-    s_c = dgated * gate_c * ogain_c_ref[...]
-    dmixed = (
-        s_c - mean_all(s_c, width) - normal_c * mean_all(s_c * normal_c, width)
-    ) * spread_c
-    diag = jnp.concatenate([jnp.where(sub == h, dmixed, 0.0) for h in range(8)], axis=1)
-    hi = diag.astype(BF16)
-    lo = (diag - hi.astype(F32)).astype(BF16)
-    w2 = jnp.concatenate([w_last.astype(F32), w_last.astype(F32)], axis=0).astype(BF16)
-    hilo = jnp.concatenate([hi.astype(F32), lo.astype(F32)], axis=0).astype(BF16)
-    dval_ref[...] = dot(w2, hilo, 0, 0)
-
-    out_dval = pltpu.make_async_copy(dval_ref, dval_out.at[0], out_sem.at[2])
-    out_dval.start()
+    small_wait(rs_buf, n_items - 1, small_recv.at[3])
+    red = de_src[i]
+    for k in range(n_items - 1):
+        red = red + rs_buf[k]
+    ar_src[...] = red
+    to_events(ar_src, ar_buf, 4)
 
     pltpu.make_async_copy(mixbuf, mixbuf, ret_rsem).wait()
     scale = 1.0 / LENGTH
@@ -538,6 +519,25 @@
 
     out_layer = pltpu.make_async_copy(layer_ref, layer_out.at[0], out_sem.at[0])
     out_layer.start()
+
+    small_wait(ar_buf, n_events - 1, small_recv.at[4])
+    total = ar_src[...]
+    for k in range(n_events - 1):
+        total = total + ar_buf[k]
+    dgated = to_compact(dot(to_rows(total).astype(BF16), wo[...], 1, 1))
+    s_c = dgated * gate_c * ogain_c_ref[...]
+    dmixed = (
+        s_c - mean_all(s_c, width) - normal_c * mean_all(s_c * normal_c, width)
+    ) * spread_c
+    diag = jnp.concatenate([jnp.where(sub == h, dmixed, 0.0) for h in range(8)], axis=1)
+    hi = diag.astype(BF16)
+    lo = (diag - hi.astype(F32)).astype(BF16)
+    w2 = jnp.concatenate([w_last.astype(F32), w_last.astype(F32)], axis=0).astype(BF16)
+    hilo = jnp.concatenate([hi.astype(F32), lo.astype(F32)], axis=0).astype(BF16)
+    dval_ref[...] = dot(w2, hilo, 0, 0)
+
+    out_dval = pltpu.make_async_copy(dval_ref, dval_out.at[0], out_sem.at[2])
+    out_dval.start()
 
     small_wait(last_buf, n_events - 1, small_send.at[0])
     small_wait(part_buf, n_events - 1, small_send.at[1])
@@ -644,8 +644,9 @@
             pltpu.VMEM(small, F32),
             pltpu.VMEM((n_events - 1,) + small, F32),
             pltpu.VMEM((COMPS * ITEM_COMPS, users * LANES), F32),
-            pltpu.VMEM((ITEM_COMPS, users * 8, LANES), F32),
-            pltpu.VMEM((ITEM_COMPS, LANES, items), BF16),
+            pltpu.VMEM((users * 8, ITEM_COMPS * items), F32),
+            pltpu.VMEM((LANES, ITEM_COMPS * items), BF16),
+            pltpu.VMEM((ITEM_COMPS * items, LANES), BF16),
             dma((5,)),
             dma((5,)),
             dma(()),

time: 50.6 us -> 46.4 us (0.917)
  the two profiles are of different devices: /device:TPU:2 before, /device:TPU:1 now
where the time goes in v4:
time: 46.4 us; the launch traced here: 46.3 us
  Pallas kernels  45 us (97%)
  between operations  1.29 us (3%)
    pallas_call x1, Pallas kernels, local(): pl.pallas_call(functools.partial(kernel, n_items, n_events), out_shape=(j...  43 us
    pallas_call x1, Pallas kernels, local(): pl.pallas_call(write_out, out_shape=(jax.ShapeDtypeStruct((1, rows, width...  1.97 us

profile of v4, /device:TPU:1, one launch (start us, length us, event | category | flops | bytes accessed | tf_op | source)
XLA Modules:
  0.0 46.3 jit_solution(5208810341505992536)
XLA Ops:
  1.3 43.0 %shard_map.148 = (bf16[1,128,1024]{2,1,0:T(8,128)(2,1)}, f32[16,128]{1,0:T(8,128)}, f32[1,128,1024]{2,1,0:T(8,128)}) custom-call(s32[1]{0:T(128)S(6)} %copy.16.lengths_ref, bf16[1,128,1024]{2,1,0:T(8,128)(2,1)} %hist_in.1, s32[1,128]{1,0:T(1,128)} %actions_in.1, bf16[16,1024]{1,0:T(8,128)(2,1)} %table_in.1, f32[1,1024]{1,0:T(1,128)} %bitcast.7, ...), custom_call_target="tpu_custom_call" | custom-call | tf_op jit(solution)/shard_map/pallas_call | solution.py:597
  44.3 2.0 %shard_map.149 = (bf16[1,128,1024]{2,1,0:T(8,128)(2,1)}, f32[16,128]{1,0:T(8,128)}, f32[1,128,1024]{2,1,0:T(8,128)}) custom-call(bf16[1,128,1024]{2,1,0:T(8,128)(2,1)} %get-tuple-element.6.layer_in, f32[16,128]{1,0:T(8,128)} %get-tuple-element.7.scores_in, f32[1,128,1024]{2,1,0:T(8,128)} %get-tuple-element.8.dval_in), custom_call_target="tpu_custom_call" | custom-call | tf_op jit(solution)/shard_map/pallas_call | solution.py:682

commit v5 on v4

--- a/solution.py
+++ b/solution.py
@@ -122,6 +122,7 @@
     dref,
     items_t,
     items_n,
+    wo_t,
     small_send,
     small_recv,
     loc_sem,
@@ -304,23 +305,22 @@
 
     both = lhs[...]
     sub = iota((8, LANES), 0)
-    q_scores = jnp.zeros((8, rows), F32)
+    q_diag = []
     for c in (2, 3):
         wloads[c].wait()
         y = silu(dot(both, w[c]))
         for j in range(CHUNK // LANES):
             head = (c % 2) * (CHUNK // LANES) + j
             q_send[head] = y[:rows, cols(j)].astype(BF16)
-            q_diag = jnp.where(sub == head, y[rows : rows + 8, cols(j)], 0.0).astype(BF16)
-            q_scores = q_scores + dot(q_diag, kv_send[head, 0], 1, 1)
+            q_diag.append(jnp.where(sub == head, y[rows : rows + 8, cols(j)], 0.0))
 
     inv = width // HEADS
+    all_keys = jnp.concatenate([kv_send[head, 0] for head in range(HEADS)], axis=1)
+    all_values = jnp.concatenate([kv_send[head, 1] for head in range(HEADS)], axis=1)
+    q_scores = dot(jnp.concatenate(q_diag, axis=1).astype(BF16), all_keys, 1, 1)
     keep_col = (iota((8, rows), 1) + e * rows) < length
     w_last = jnp.where(keep_col, silu(q_scores * inv ** (-0.5)) * (1.0 / LENGTH), 0.0).astype(BF16)
-    part = jnp.zeros((8, LANES), F32)
-    for head in range(HEADS):
-        part = part + jnp.where(sub == head, dot(w_last, kv_send[head, 1]), 0.0)
-    part_src[...] = part
+    part_src[...] = to_compact(dot(w_last, all_values))
     to_events(part_src, part_buf, 1)
 
     gate_rows = []
@@ -400,6 +400,7 @@
     lax.fori_loop(1, chips, forward, 0)
 
 
+    wo_t[...] = wo[...].T
     users = n_items
     small_wait(user_buf, n_items - 1, small_recv.at[2])
     everyone = user_buf[...].reshape(users * 8, LANES).astype(BF16)
@@ -524,7 +525,7 @@
     total = ar_src[...]
     for k in range(n_events - 1):
         total = total + ar_buf[k]
-    dgated = to_compact(dot(to_rows(total).astype(BF16), wo[...], 1, 1))
+    dgated = to_compact(dot(to_rows(total).astype(BF16), wo_t[...]))
     s_c = dgated * gate_c * ogain_c_ref[...]
     dmixed = (
         s_c - mean_all(s_c, width) - normal_c * mean_all(s_c * normal_c, width)
@@ -647,6 +648,7 @@
             pltpu.VMEM((users * 8, ITEM_COMPS * items), F32),
             pltpu.VMEM((LANES, ITEM_COMPS * items), BF16),
             pltpu.VMEM((ITEM_COMPS * items, LANES), BF16),
+            pltpu.VMEM((width, width), BF16),
             dma((5,)),
             dma((5,)),
             dma(()),

time: 46.4 us -> 46.1 us (level)
  no operation moved by 1% of the time
where the time goes in v5:
time: 46.1 us; the launch traced here: 46 us
  Pallas kernels  44.7 us (97%)
  between operations  1.29 us (3%)
    pallas_call x1, Pallas kernels, local(): pl.pallas_call(functools.partial(kernel, n_items, n_events), out_shape=(j...  42.7 us
    pallas_call x1, Pallas kernels, local(): pl.pallas_call(write_out, out_shape=(jax.ShapeDtypeStruct((1, rows, width...  1.97 us

profile of v5, /device:TPU:1, one launch (start us, length us, event | category | flops | bytes accessed | tf_op | source)
XLA Modules:
  0.0 46.0 jit_solution(4280364036912291047)
XLA Ops:
  1.3 42.7 %shard_map.148 = (bf16[1,128,1024]{2,1,0:T(8,128)(2,1)}, f32[16,128]{1,0:T(8,128)}, f32[1,128,1024]{2,1,0:T(8,128)}) custom-call(s32[1]{0:T(128)S(6)} %copy.16.lengths_ref, bf16[1,128,1024]{2,1,0:T(8,128)(2,1)} %hist_in.1, s32[1,128]{1,0:T(1,128)} %actions_in.1, bf16[16,1024]{1,0:T(8,128)(2,1)} %table_in.1, f32[1,1024]{1,0:T(1,128)} %bitcast.7, ...), custom_call_target="tpu_custom_call" | custom-call | tf_op jit(solution)/shard_map/pallas_call | solution.py:598
  44.0 2.0 %shard_map.149 = (bf16[1,128,1024]{2,1,0:T(8,128)(2,1)}, f32[16,128]{1,0:T(8,128)}, f32[1,128,1024]{2,1,0:T(8,128)}) custom-call(bf16[1,128,1024]{2,1,0:T(8,128)(2,1)} %get-tuple-element.6.layer_in, f32[16,128]{1,0:T(8,128)} %get-tuple-element.7.scores_in, f32[1,128,1024]{2,1,0:T(8,128)} %get-tuple-element.8.dval_in), custom_call_target="tpu_custom_call" | custom-call | tf_op jit(solution)/shard_map/pallas_call | solution.py:684
